TPU v7x, 128 devices: a whole 4x4x4 slice. The times are simulated.
128 devices in a mesh: ctx: 32 (over x, z, core), tp: 4 (over y).
Axes of the slice: x: 4, y: 4, z: 4, core: 2. Of those that a mesh axis runs over, the one named last changes fastest.
Arguments:
- queries: bfloat16 [16384, 4096], P('ctx', 'tp'), may hold values from -160 to 160
- slot_table: int32 [256, 4], P('ctx'), may hold values from -1 to 831, as said below
- states: bfloat16 [832, 128, 512], P('ctx'), may hold values from -6 to 6
- key_weight: bfloat16 [512, 4096], P(None, 'tp'), may hold values from -0.25 to 0.25
- value_weight: bfloat16 [512, 4096], P(None, 'tp'), may hold values from -0.25 to 0.25
- out_grad: bfloat16 [16384, 4096], P('ctx', 'tp'), may hold values from -6 to 6
Outputs:
- attended: bfloat16 [16384, 4096], P('ctx', 'tp')
- query_grad: bfloat16 [16384, 4096], P('ctx', 'tp')
- states_grad: bfloat16 [832, 128, 512], P('ctx', None, 'tp')
- key_weight_grad: float32 [512, 4096], P('ctx', 'tp')
- value_weight_grad: float32 [512, 4096], P('ctx', 'tp')
Inputs may be any that keep to these rules, and one draw needn't show every extreme that they name: `slot_table`: row c of the table lists the slots of stretch c's neighbours: 1 to 4 slot numbers first, then -1; one row in every draw has 4. Every slot appears exactly once. Of the neighbours of one device's 8 stretches, at most 2 are stored in the slots of any one device, and that many in some pair of devices in every draw.
All inputs are finite; a program needn't handle non-finite values.
Results may differ from a plain program's by a relative error of at most 0.023.
The roundings to bfloat16 on the way count: a program that leaves them out, or rounds other values in their place, can miss the bound.
Values may be sent and summed in bfloat16 or wider, within the bound.
No kernel may reach another device: no remote copies, remote signals or barrier semaphores. Data moves between devices by JAX's collectives and lax.ppermute only.
A program may use at most 192 MiB of HBM per device.

v0:
```python
import jax
import jax.numpy as jnp
from jax import lax
from jax.sharding import PartitionSpec as P

HEAD_DIM = 128


def owner_ranks(table, slots_dev):
    present = table >= 0
    owners = jnp.where(present, table // slots_dev, -1)
    positions = jnp.arange(table.shape[-1])
    before = positions[None, :] < positions[:, None]
    alike = (owners[..., :, None] == owners[..., None, :]) & present[..., None, :] & before
    ranks = jnp.sum(alike.astype(jnp.int32), axis=-1)
    return (present, owners, ranks)


def body(queries, slot_table, states, key_weight, value_weight, out_grad):
    devices = lax.axis_size("ctx")
    stretches_dev, neighbours = slot_table.shape
    slots_dev, span, enc_width = states.shape
    capacity = max(2, (neighbours * stretches_dev + devices - 2) // (devices - 1))
    my_index = lax.axis_index("ctx")
    tables = lax.all_gather(slot_table, "ctx", axis=0, tiled=True)
    every = tables.reshape(devices, stretches_dev * neighbours)
    live_all, owners_all, ranks_all = owner_ranks(every, slots_dev)
    choose = (owners_all == my_index)[:, :, None] & (
        ranks_all[:, :, None] == jnp.arange(capacity)[None, None, :]
    )
    local_slot = jnp.sum(jnp.where(choose, (every % slots_dev)[:, :, None], 0), axis=1)
    sending = jnp.any(choose, axis=1).reshape(-1)
    send_rows = jnp.where(sending, local_slot.reshape(-1), 0)
    place_rows = jnp.where(sending, local_slot.reshape(-1), slots_dev)
    live, own_owner, own_rank = owner_ranks(slot_table.reshape(-1), slots_dev)
    recv_rows = jnp.where(live, own_owner * capacity + own_rank, 0)
    back_rows = jnp.where(live, own_owner * capacity + own_rank, devices * capacity)
    picked = jnp.take(states, send_rows, axis=0)
    picked = jnp.where(sending[:, None, None], picked, jnp.zeros_like(picked))
    arrived = lax.all_to_all(
        picked.reshape(devices, capacity, span, states.shape[2]),
        "ctx",
        split_axis=0,
        concat_axis=0,
        tiled=True,
    )
    arrived = arrived.reshape(devices * capacity, span, enc_width)
    gathered = jnp.take(arrived, recv_rows, axis=0)
    gathered = jnp.where(live[:, None, None], gathered, jnp.zeros_like(gathered))
    flat = gathered.reshape(-1, enc_width)
    width_dev = key_weight.shape[1]
    heads_dev = width_dev // HEAD_DIM
    scale = HEAD_DIM ** (-0.5)
    stretch_len = queries.shape[0] // stretches_dev
    keys = jnp.dot(flat, key_weight, preferred_element_type=jnp.float32).astype(jnp.bfloat16)
    values = jnp.dot(flat, value_weight, preferred_element_type=jnp.float32).astype(jnp.bfloat16)
    keys = keys.reshape(stretches_dev, neighbours * span, heads_dev, HEAD_DIM)
    values = values.reshape(stretches_dev, neighbours * span, heads_dev, HEAD_DIM)
    query = queries.reshape(stretches_dev, stretch_len, heads_dev, HEAD_DIM)
    dout = out_grad.reshape(stretches_dev, stretch_len, heads_dev, HEAD_DIM)
    mask = jnp.repeat(live.reshape(stretches_dev, neighbours), span, axis=1)[:, None, None, :]
    scores = jnp.einsum("cqhd,ckhd->chqk", query, keys, preferred_element_type=jnp.float32) * scale
    scores = jnp.where(mask, scores, -jnp.inf)
    top = jnp.max(scores, axis=-1, keepdims=True)
    expo = jnp.exp(scores - top)
    probs = expo / jnp.sum(expo, axis=-1, keepdims=True)
    probs_b = probs.astype(jnp.bfloat16)
    attended = jnp.einsum(
        "chqk,ckhd->cqhd", probs_b, values, preferred_element_type=jnp.float32
    ).astype(jnp.bfloat16)
    dprobs = jnp.einsum("cqhd,ckhd->chqk", dout, values, preferred_element_type=jnp.float32)
    dscores = probs * (dprobs - jnp.sum(probs * dprobs, axis=-1, keepdims=True))
    dscores_b = dscores.astype(jnp.bfloat16)
    query_grad = (
        jnp.einsum("chqk,ckhd->cqhd", dscores_b, keys, preferred_element_type=jnp.float32) * scale
    ).astype(jnp.bfloat16)
    key_grad = (
        jnp.einsum("chqk,cqhd->ckhd", dscores_b, query, preferred_element_type=jnp.float32) * scale
    ).astype(jnp.bfloat16)
    value_grad = jnp.einsum(
        "chqk,cqhd->ckhd", probs_b, dout, preferred_element_type=jnp.float32
    ).astype(jnp.bfloat16)
    key_grad = key_grad.reshape(-1, width_dev)
    value_grad = value_grad.reshape(-1, width_dev)
    over_rows = (((0,), (0,)), ((), ()))
    key_terms = lax.dot_general(flat, key_grad, over_rows, preferred_element_type=jnp.float32)
    value_terms = lax.dot_general(flat, value_grad, over_rows, preferred_element_type=jnp.float32)
    key_weight_grad, value_weight_grad = (
        lax.psum_scatter(
            key_terms.astype(jnp.bfloat16), "ctx", scatter_dimension=0, tiled=True
        ).astype(jnp.float32),
        lax.psum_scatter(
            value_terms.astype(jnp.bfloat16), "ctx", scatter_dimension=0, tiled=True
        ).astype(jnp.float32),
    )
    over_cols = (((1,), (1,)), ((), ()))
    partial_sum = lax.dot_general(
        key_grad, key_weight, over_cols, preferred_element_type=jnp.float32
    )
    partial_sum = partial_sum + lax.dot_general(
        value_grad, value_weight, over_cols, preferred_element_type=jnp.float32
    )
    partial_sum = partial_sum.reshape(stretches_dev * neighbours, span, enc_width)
    summed = lax.psum_scatter(
        partial_sum.astype(jnp.bfloat16), "tp", scatter_dimension=2, tiled=True
    )
    part_width = summed.shape[2]
    leaving = (
        jnp.zeros((devices * capacity, span, part_width), jnp.bfloat16)
        .at[back_rows]
        .set(summed, mode="drop")
    )
    landed = lax.all_to_all(
        leaving.reshape(devices, capacity, span, part_width),
        "ctx",
        split_axis=0,
        concat_axis=0,
        tiled=True,
    )
    landed = landed.reshape(devices * capacity, span, part_width)
    states_grad = (
        jnp.zeros((slots_dev, span, part_width), jnp.bfloat16)
        .at[place_rows]
        .set(landed, mode="drop")
    )
    attended = attended.reshape(stretches_dev * stretch_len, width_dev)
    query_grad = query_grad.reshape(stretches_dev * stretch_len, width_dev)
    return (attended, query_grad, states_grad, key_weight_grad, value_weight_grad)


def solution(mesh):
    in_specs = (
        P("ctx", "tp"),
        P("ctx", None),
        P("ctx", None, None),
        P(None, "tp"),
        P(None, "tp"),
        P("ctx", "tp"),
    )
    out_specs = (
        P("ctx", "tp"),
        P("ctx", "tp"),
        P("ctx", None, "tp"),
        P("ctx", "tp"),
        P("ctx", "tp"),
    )
    return jax.shard_map(body, mesh=mesh, in_specs=in_specs, out_specs=out_specs, check_vma=False)
```

profile of v0, /device:TPU:1, one launch (start us, length us, event | category | flops | bytes accessed | tf_op | source)
XLA Modules:
  0.0 563.1 jit_solution(12766338169353697185)
XLA Ops:
  7.2 27.1 %all-gather = s32[32,8,4]{1,2,0:T(4,128)S(1)} all-gather(s32[1,8,4]{1,2,0:T(4,128)} %bitcast.154), channel_id=1, replica_groups=mesh['ctx'=32,'tp'=4] {'ctx'}, dimensions={0}, use_global_device_ids=true | all-gather | bytes 4224 | tf_op jit(solution)/shard_map/all_gather | solution.py:25
  36.3 5.5 gather_fusion
  41.8 7.6 %select_select_fusion = bf16[32,2,128,512]{3,2,1,0:T(8,128)(2,1)} fusion(bf16[32,2,128,512]{3,2,1,0:T(8,128)(2,1)} %bitcast.125, pred[32,2]{1,0:T(8,128)(4,1)S(1)} %copy.127, pred[32,2]{1,0:T(8,128)(4,1)S(1)} %copy.125), kind=kLoop, calls=%fused_computation.28 | loop fusion | flops 8388608 | bytes 16777344 | tf_op jit(solution)/shard_map/jit(_where)/select_n | solution.py:39
  49.4 5.3 all-to-all-start
  56.8 106.5 %all-to-all-done = bf16[32,2,128,512]{3,2,1,0:T(8,128)(2,1)} async-done(((bf16[32,2,128,512]{3,2,1,0:T(8,128)(2,1)}), bf16[32,2,128,512]{3,2,1,0:T(8,128)(2,1)}, u32[]{:S(2)}, u32[]{:S(2)}) %all-to-all-start) | async-done | bytes 8388640 | tf_op jit(solution)/shard_map/all_to_all | solution.py:40
  163.3 6.1 %gather_fusion.1 = bf16[32,128,512]{2,1,0:T(8,128)(2,1)} fusion(bf16[64,128,512]{2,1,0:T(8,128)(2,1)} %bitcast.9, s32[1024]{0:T(1024)S(1)} %pad_clamp_fusion), kind=kCustom, calls=%fused_computation.1 | custom fusion | bytes 8388736 | tf_op jit(solution)/shard_map/jit(_take)/gather | solution.py:48
  169.4 5.3 fusion.31
  176.7 6.6 %convert_bitcast_fusion.2 = bf16[512,8,8,128]{3,1,2,0:T(8,128)(2,1)} fusion(bf16[4096,512]{1,0:T(8,128)(2,1)S(1)} %fusion.31, bf16[512,1024]{1,0:T(8,128)(2,1)S(1)} %copy-done.10), kind=kOutput, calls=%fused_computation.27 | convolution fusion | flops 4299161600 | bytes 13631488 | tf_op jit(solution)/shard_map/dot_general | solution.py:56
  183.4 8.9 %copy.149 = bf16[512,8,8,128]{3,2,1,0:T(8,128)(2,1)} copy(bf16[512,8,8,128]{3,1,2,0:T(8,128)(2,1)} %convert_bitcast_fusion.2) | data formatting | bytes 16777216
  192.2 9.1 %convert_bitcast_fusion.1 = bf16[512,8,8,128]{3,1,2,0:T(8,128)(2,1)} fusion(bf16[4096,512]{1,0:T(8,128)(2,1)} %copy-done.5, bf16[512,1024]{1,0:T(8,128)(2,1)S(1)} %copy-done.12), kind=kOutput, calls=%fused_computation.26 | convolution fusion | flops 4299161600 | bytes 13631488 | tf_op jit(solution)/shard_map/dot_general | solution.py:55
  201.4 8.8 %copy.147 = bf16[512,8,8,128]{3,2,1,0:T(8,128)(2,1)} copy(bf16[512,8,8,128]{3,1,2,0:T(8,128)(2,1)} %convert_bitcast_fusion.1) | data formatting | bytes 16777216
  210.1 9.6 %fusion.24 = f32[8,8,512,64]{2,3,1,0:T(8,128)} fusion(bf16[8,512,8,128]{3,2,1,0:T(8,128)(2,1)} %bitcast.123, bf16[8,64,8,128]{3,2,1,0:T(8,128)(2,1)S(1)} %bitcast.128), kind=kOutput, calls=%fused_computation.39 | convolution fusion | flops 536870912 | bytes 17825792 | tf_op jit(solution)/shard_map/cqhd,ckhd->chqk/dot_general | solution.py:62
  219.8 11.2 %fusion.75 = (f32[8,8,64]{2,1,0:T(8,128)S(1)}, f32[8,8,64,512]{3,2,1,0:T(8,128)}) fusion(f32[8,8,512,64]{2,3,1,0:T(8,128)} %fusion.24, pred[8,512]{1,0:T(8,128)(4,1)S(1)} %broadcast_bitcast_fusion), kind=kOutput, calls=%fused_computation.111 | output fusion | flops 12583423 | bytes 16797696 | tf_op jit(solution)/shard_map/sub | solution.py:65
  231.0 7.7 %convert_bitcast_fusion = bf16[8,512,8,128]{3,1,2,0:T(8,128)(2,1)} fusion(bf16[8,64,8,128]{3,2,1,0:T(8,128)(2,1)S(1)} %bitcast.144, f32[8,8,64,512]{3,2,1,0:T(8,128)} %get-tuple-element.18, f32[8,8,64]{2,1,0:T(8,128)S(1)} %get-tuple-element.17), kind=kOutput, calls=%fused_computation.24 | convolution fusion | flops 545259520 | bytes 17842176 | tf_op jit(solution)/shard_map/chqk,cqhd->ckhd/dot_general | solution.py:80
  238.6 10.0 %fusion.9 = (f32[8,8,64]{2,1,0:T(8,128)S(1)}, f32[8,8,512,64]{2,3,1,0:T(8,128)}) fusion(f32[8,8,64,512]{3,2,1,0:T(8,128)} %get-tuple-element.18, f32[8,8,64]{2,1,0:T(8,128)S(1)} %get-tuple-element.17, bf16[8,64,8,128]{3,2,1,0:T(8,128)(2,1)S(1)} %bitcast.145, bf16[8,512,8,128]{3,2,1,0:T(8,128)(2,1)} %bitcast.130), kind=kOutput, calls=%fused_computation.16 | convolution fusion | flops 543158272 | bytes 26247168 | tf_op jit(solution)/shard_map/cqhd,ckhd->chqk/dot_general | solution.py:71
  248.7 12.1 %copy.144 = bf16[8,512,8,128]{3,2,1,0:T(8,128)(2,1)} copy(bf16[8,512,8,128]{3,1,2,0:T(8,128)(2,1)} %convert_bitcast_fusion) | data formatting | bytes 16777216 | tf_op jit(solution)/shard_map/convert_element_type | solution.py:82
  260.8 10.4 %fusion.3 = f32[4096,512]{1,0:T(8,128)} fusion(bf16[512,1024]{1,0:T(8,128)(2,1)S(1)} %copy-done.11, bf16[512,8,8,128]{3,2,1,0:T(8,128)(2,1)} %bitcast.132), kind=kOutput, calls=%fused_computation.8 | convolution fusion | flops 4294967296 | bytes 17825792 | tf_op jit(solution)/shard_map/dot_general | solution.py:100
  277.3 5.1 fusion.28
  282.5 12.1 %copy.142 = bf16[8,512,8,128]{3,2,1,0:T(8,128)(2,1)} copy(bf16[8,512,8,128]{3,1,2,0:T(8,128)(2,1)} %fusion.28) | data formatting | bytes 16777216 | tf_op jit(solution)/shard_map/convert_element_type | solution.py:79
  294.5 10.8 %add_convert_fusion = bf16[4096,512]{1,0:T(8,128)(2,1)} fusion(f32[4096,512]{1,0:T(8,128)} %fusion.3, bf16[512,1024]{1,0:T(8,128)(2,1)S(1)} %copy-done.13, bf16[512,8,8,128]{3,2,1,0:T(8,128)(2,1)} %bitcast.134), kind=kOutput, calls=%fused_computation.23 | convolution fusion | flops 4299161600 | bytes 22020096 | tf_op jit(solution)/shard_map/dot_general | solution.py:97
  305.3 8.1 %copy.145 = bf16[32,128,512]{1,0,2:T(8,128)(2,1)} copy(bf16[32,128,512]{2,1,0:T(8,128)(2,1)} %bitcast.138) | data formatting | bytes 8388608
  313.5 8.3 %copy.210 = bf16[64,8,32,128]{3,1,2,0:T(8,128)(2,1)} copy(bf16[64,8,32,128]{3,2,1,0:T(8,128)(2,1)} %bitcast.127) | data formatting | bytes 8388608
  326.7 8.2 %fusion.44 = bf16[512,1024]{1,0:T(8,128)(2,1)} fusion(bf16[4096,512]{1,0:T(8,128)(2,1)S(1)} %bitcast.136, bf16[512,8,8,128]{3,2,1,0:T(8,128)(2,1)} %bitcast.135), kind=kOutput, calls=%fused_computation.54 | convolution fusion | flops 4295491584 | bytes 13631488 | tf_op jit(solution)/shard_map/dot_general | solution.py:86
  334.9 10.1 %fusion.47 = bf16[512,1024]{1,0:T(8,128)(2,1)} fusion(bf16[4096,512]{1,0:T(8,128)(2,1)} %bitcast.137, bf16[512,8,8,128]{3,2,1,0:T(8,128)(2,1)} %bitcast.133), kind=kOutput, calls=%fused_computation.55 | convolution fusion | flops 4295491584 | bytes 13631488 | tf_op jit(solution)/shard_map/dot_general | solution.py:87
  345.1 38.9 %reduce-scatter.10.cloned.1.call-done = bf16[128,4096]{1,0:T(8,128)(2,1)} async-done(((bf16[512,4096]{1,0:T(8,128)(2,1)}), bf16[128,4096]{1,0:T(8,128)(2,1)}) %reduce-scatter.10.cloned.1.call-update) | async-done | bytes 1048592
  388.5 4.7 scatter_fusion
  393.3 7.5 %all-to-all-start.1 = ((bf16[32,2,128,128]{3,2,1,0:T(8,128)(2,1)}), bf16[32,2,128,128]{3,2,1,0:T(8,128)(2,1)}, u32[]{:S(2)}, u32[]{:S(2)}) async-start(bf16[32,2,128,128]{3,2,1,0:T(8,128)(2,1)} %bitcast.23), calls=%async_computation.1 | async-start | bytes 4194304 | tf_op jit(solution)/shard_map/all_to_all | solution.py:113
  400.8 8.5 %fusion.50 = bf16[8,64,8,128]{3,1,2,0:T(8,128)(2,1)S(1)} fusion(bf16[8,512,8,128]{3,2,1,0:T(8,128)(2,1)} %bitcast.131, f32[8,8,64,512]{3,2,1,0:T(8,128)} %get-tuple-element.18, f32[8,8,64]{2,1,0:T(8,128)S(1)} %get-tuple-element.17), kind=kOutput, calls=%fused_computation.56 | convolution fusion | flops 541589504 | bytes 17842176 | tf_op jit(solution)/shard_map/chqk,ckhd->cqhd/dot_general | solution.py:68
  411.2 5.5 fusion.55
  418.7 45.0 %reduce-scatter.6.cloned.1.call-done = bf16[16,1024]{1,0:T(8,128)(2,1)} async-done(((bf16[512,1024]{1,0:T(8,128)(2,1)}), bf16[16,1024]{1,0:T(8,128)(2,1)}) %reduce-scatter.6.cloned.1.call-update) | async-done | bytes 32784 | tf_op jit(solution)/shard_map/reduce_scatter | solution.py:89
  465.0 79.0 %reduce-scatter.8.cloned.1.call-done = bf16[16,1024]{1,0:T(8,128)(2,1)} async-done(((bf16[512,1024]{1,0:T(8,128)(2,1)}), bf16[16,1024]{1,0:T(8,128)(2,1)}) %reduce-scatter.8.cloned.1.call-update) | async-done | bytes 32784 | tf_op jit(solution)/shard_map/reduce_scatter | solution.py:92
  546.5 9.8 %scatter_fusion.1 = bf16[26,128,128]{2,1,0:T(8,128)(2,1)} fusion(bf16[26,128,128]{2,1,0:T(8,128)(2,1)} %broadcast_in_dim.147, s32[64]{0:T(128)S(1)} %fusion.70, bf16[64,128,128]{2,1,0:T(8,128)(2,1)} %bitcast.24), kind=kCustom, calls=%fused_computation.3 | custom fusion | bytes 6291712 | tf_op jit(solution)/shard_map/scatter | solution.py:124
  (96 shorter events, 29.2 us)
Async XLA Ops:
  7.2 29.1 %copy-start = (bf16[26,128,512]{2,1,0:T(8,128)(2,1)S(1)}, bf16[26,128,512]{2,1,0:T(8,128)(2,1)}, u32[]{:S(2)}) copy-start(bf16[26,128,512]{2,1,0:T(8,128)(2,1)} %param.8) | copy-start | bytes 10223620
  49.4 5.6 copy-start.9
  49.4 6.4 %copy-start.7 = (bf16[512,1024]{1,0:T(8,128)(2,1)S(1)}, bf16[512,1024]{1,0:T(8,128)(2,1)}, u32[]{:S(2)}) copy-start(bf16[512,1024]{1,0:T(8,128)(2,1)} %param.6) | copy-start | bytes 3145732
  49.4 6.7 %copy-start.8 = (bf16[512,1024]{1,0:T(8,128)(2,1)S(1)}, bf16[512,1024]{1,0:T(8,128)(2,1)}, u32[]{:S(2)}) copy-start(bf16[512,1024]{1,0:T(8,128)(2,1)} %param.11) | copy-start | bytes 3145732
  49.4 113.9 %all-to-all-start = ((bf16[32,2,128,512]{3,2,1,0:T(8,128)(2,1)}), bf16[32,2,128,512]{3,2,1,0:T(8,128)(2,1)}, u32[]{:S(2)}, u32[]{:S(2)}) async-start(bf16[32,2,128,512]{3,2,1,0:T(8,128)(2,1)} %select_select_fusion), calls=%async_computation | async-start | bytes 16777216 | tf_op jit(solution)/shard_map/all_to_all | solution.py:40
  54.7 329.3 %reduce-scatter.10.cloned.1.call-start = ((), (), s32[]{:S(2)}) async-start(), calls=%async_computation.7 | async-start | bytes 5242880
  169.4 7.3 %copy-start.10 = (bf16[512,1024]{1,0:T(8,128)(2,1)S(1)}, bf16[512,1024]{1,0:T(8,128)(2,1)}, u32[]{:S(2)}) copy-start(bf16[512,1024]{1,0:T(8,128)(2,1)} %param.10) | copy-start | bytes 3145732
  174.7 2.0 copy-start.5
  183.3 8.9 %copy-start.12 = (bf16[512,1024]{1,0:T(8,128)(2,1)S(1)}, bf16[512,1024]{1,0:T(8,128)(2,1)}, u32[]{:S(2)}) copy-start(bf16[512,1024]{1,0:T(8,128)(2,1)} %param.9) | copy-start | bytes 3145732
  248.7 12.1 %copy-start.11 = (bf16[512,1024]{1,0:T(8,128)(2,1)S(1)}, bf16[512,1024]{1,0:T(8,128)(2,1)}, u32[]{:S(2)}) copy-start(bf16[512,1024]{1,0:T(8,128)(2,1)} %param.10) | copy-start | bytes 3145732
  260.8 10.4 %copy-start.4 = (f32[8,8,512,64]{2,3,1,0:T(8,128)S(1)}, f32[8,8,512,64]{2,3,1,0:T(8,128)}, u32[]{:S(2)}) copy-start(f32[8,8,512,64]{2,3,1,0:T(8,128)} %get-tuple-element.20) | copy-start | bytes 25165828
  275.4 1.9 copy-start.2
  282.4 12.1 %copy-start.13 = (bf16[512,1024]{1,0:T(8,128)(2,1)S(1)}, bf16[512,1024]{1,0:T(8,128)(2,1)}, u32[]{:S(2)}) copy-start(bf16[512,1024]{1,0:T(8,128)(2,1)} %param.9) | copy-start | bytes 3145732
  321.8 141.9 %reduce-scatter.6.cloned.1.call-start = ((), (), s32[]{:S(2)}) async-start(), calls=%async_computation.5 | async-start | bytes 1081344 | tf_op jit(solution)/shard_map/reduce_scatter | solution.py:89
  324.7 1.9 copy-start.6
  334.9 209.1 %reduce-scatter.8.cloned.1.call-start = ((), (), s32[]{:S(2)}) async-start(), calls=%async_computation.6 | async-start | bytes 1081344 | tf_op jit(solution)/shard_map/reduce_scatter | solution.py:92
  393.3 152.2 %all-to-all-start.1 = ((bf16[32,2,128,128]{3,2,1,0:T(8,128)(2,1)}), bf16[32,2,128,128]{3,2,1,0:T(8,128)(2,1)}, u32[]{:S(2)}, u32[]{:S(2)}) async-start(bf16[32,2,128,128]{3,2,1,0:T(8,128)(2,1)} %bitcast.23), calls=%async_computation.1 | async-start | bytes 4194304 | tf_op jit(solution)/shard_map/all_to_all | solution.py:113
  400.8 10.5 %copy-start.3 = (bf16[8,8,64,512]{3,2,1,0:T(8,128)(2,1)S(1)}, bf16[8,8,64,512]{3,2,1,0:T(8,128)(2,1)}, u32[]{:S(2)}) copy-start(bf16[8,8,64,512]{3,2,1,0:T(8,128)(2,1)} %copy-done.2) | copy-start | bytes 12582916
  411.2 145.1 %copy-start.1 = (bf16[26,128,512]{2,1,0:T(8,128)(2,1)S(1)}, bf16[26,128,512]{2,1,0:T(8,128)(2,1)}, u32[]{:S(2)}) copy-start(bf16[26,128,512]{2,1,0:T(8,128)(2,1)} %param.8) | copy-start | bytes 10223620
Sparse Core Ops, SparseCore 0:
  321.9 62.0 reduce-scatter.9
  387.9 75.6 reduce-scatter.5
  467.1 76.8 reduce-scatter.7
where the time goes:
time: 569 us; the launch traced here: 563 us
  waiting for transfers between devices  269 us (47%)
  local copies, waits for them, and re-layouts  102 us (18%)
  matrix products  102 us (18%)
  other arithmetic  35.2 us (6%)
  blocking collectives  27.1 us (5%)
  between operations  14.4 us (3%)
  starting transfers between devices  13.1 us (2%)
    all_to_all x1, waiting for transfers between devices, body(): lax.all_to_all(picked.reshape(devices, capacity, span, states.shape[2]),...  106 us
    reduce_scatter x1, waiting for transfers between devices, body(): lax.psum_scatter(value_terms.astype(jnp.bfloat16), 'ctx', scatter_dimensi...  79 us
    unnamed x38, local copies, waits for them, and re-layouts  45.6 us
    reduce_scatter x1, waiting for transfers between devices, body(): lax.psum_scatter(key_terms.astype(jnp.bfloat16), 'ctx', scatter_dimension...  45 us
    unnamed x4, waiting for transfers between devices  38.9 us
    all_gather x1, blocking collectives, body(): tables = lax.all_gather(slot_table, 'ctx', axis=0, tiled=True)  27.1 us
    convert_element_type x1, local copies, waits for them, and re-layouts, body(): value_grad = jnp.einsum('chqk,cqhd->ckhd', probs_b, dout, preferred_eleme...  12.1 us
    convert_element_type x1, local copies, waits for them, and re-layouts, body(): key_grad = (jnp.einsum('chqk,cqhd->ckhd', dscores_b, query, preferred_ele...  12.1 us
  transfers between devices with their start and end apart: 5, of which 4 were waited for; matrix products, arithmetic and copies ran while one was open for 9% of the time, Pallas kernels for 0%

commit v1 on v0

v1 whole, which is shorter than its diff:
```python
import functools

import jax
import jax.numpy as jnp
from jax import lax
from jax.experimental import pallas as pl
from jax.experimental.pallas import tpu as pltpu
from jax.sharding import PartitionSpec as P

HEAD_DIM = 128
CHUNK = 4
F32 = jnp.float32
BF16 = jnp.bfloat16
NN = (((1,), (0,)), ((), ()))
NT = (((1,), (1,)), ((), ()))
TN = (((0,), (0,)), ((), ()))
MIB = 2**20


def dot(a, b, dims=NN):
    return lax.dot_general(a, b, dims, preferred_element_type=F32)


def attend_kernel(counts, s0, s1, s2, s3, w, wt, q_ref, do_ref, *rest, heads, span, first):
    att, qg, grads, p0, p1, p2, p3, kv = rest[-8:]
    c = pl.program_id(0)
    width = heads * HEAD_DIM
    scale = HEAD_DIM ** (-0.5)
    rows = s0.shape[0]
    length = q_ref.shape[0]
    states = jnp.concatenate([s0[...], s1[...], s2[...], s3[...]], axis=1)
    kv[...] = dot(states, w[...]).astype(BF16)
    mask = lax.broadcasted_iota(jnp.int32, (rows, 1), 0) < counts[first + c] * span
    zero = jnp.zeros((length, HEAD_DIM), BF16)

    def spread(ref, lo):
        top = jnp.concatenate([ref[:, lo : lo + HEAD_DIM], zero], axis=1)
        low = jnp.concatenate([zero, ref[:, lo + HEAD_DIM : lo + 2 * HEAD_DIM]], axis=1)
        return jnp.concatenate([top, low], axis=0)

    for h in range(0, heads, 2):
        lo = h * HEAD_DIM
        mid, hi = lo + HEAD_DIM, lo + 2 * HEAD_DIM
        q = spread(q_ref, lo)
        do = spread(do_ref, lo)
        k = kv[:, lo:hi]
        v = kv[:, width + lo : width + hi]
        scores = jnp.where(mask, dot(k, q, NT), -jnp.inf)
        dprobs = dot(v, do, NT)
        expo = jnp.exp((scores - jnp.max(scores, axis=0, keepdims=True)) * scale)
        probs = expo * (1.0 / jnp.sum(expo, axis=0, keepdims=True))
        dscores = probs * (dprobs - jnp.sum(probs * dprobs, axis=0, keepdims=True))
        probs_b = probs.astype(BF16)
        dscores_b = dscores.astype(BF16)
        grads[:, width + lo : width + hi] = dot(probs_b, do).astype(BF16)
        grads[:, lo:hi] = (dot(dscores_b, q) * scale).astype(BF16)
        both = dot(probs_b, v, TN).astype(BF16)
        att[:, lo:mid] = both[:length, :HEAD_DIM]
        att[:, mid:hi] = both[length:, HEAD_DIM:]
        both = (dot(dscores_b, k, TN) * scale).astype(BF16)
        qg[:, lo:mid] = both[:length, :HEAD_DIM]
        qg[:, mid:hi] = both[length:, HEAD_DIM:]
    part = dot(grads[...], wt[...]).astype(BF16)
    n = p0.shape[1]
    p0[...] = part[:, :n]
    p1[...] = part[:, n : 2 * n]
    p2[...] = part[:, 2 * n : 3 * n]
    p3[...] = part[:, 3 * n :]


def attend(counts, pieces, w, wt, q, do, after, first, number, span):
    heads = q.shape[1] // HEAD_DIM
    stretches = counts.shape[0]
    length = q.shape[0] // stretches
    width = q.shape[1]
    rows = pieces[0].shape[0] // number
    part = pieces[0].shape[1]
    piece = pl.BlockSpec((rows, part), lambda c, n: (c, 0))
    token = pl.BlockSpec((length, width), lambda c, n: (first + c, 0))
    whole = pl.BlockSpec((rows, 2 * width), lambda c, n: (c, 0))
    token_out = pl.BlockSpec((length, width), lambda c, n: (c, 0))
    anywhere = pl.BlockSpec(memory_space=pl.ANY)

    def fixed(a):
        return pl.BlockSpec(a.shape, lambda c, n: (0, 0), pipeline_mode=pl.Buffered(1))

    shape = jax.ShapeDtypeStruct
    return pl.pallas_call(
        functools.partial(attend_kernel, heads=heads, span=span, first=first),
        grid_spec=pltpu.PrefetchScalarGridSpec(
            num_scalar_prefetch=1,
            grid=(number,),
            in_specs=[piece] * 4 + [fixed(w), fixed(wt), token, token] + [anywhere] * len(after),
            out_specs=[token_out, token_out, whole] + [piece] * 4,
            scratch_shapes=[pltpu.VMEM((rows, 2 * width), BF16)],
        ),
        out_shape=[shape((number * length, width), BF16)] * 2
        + [shape((number * rows, 2 * width), BF16)]
        + [shape((number * rows, part), BF16)] * 4,
        compiler_params=pltpu.CompilerParams(vmem_limit_bytes=60 * MIB),
        cost_estimate=pl.CostEstimate(
            flops=number * 6_000_000_000, bytes_accessed=4_000_000, transcendentals=0
        ),
    )(counts, *pieces, w, wt, q, do, *after)


def weights_kernel(quarters, *refs, chunks):
    pieces, grads = refs[: 4 * chunks], refs[4 * chunks : 5 * chunks]
    out, turned = refs[-2:]
    part = pieces[0].shape[1]
    rows = pieces[0].shape[0]

    @pl.when(pl.program_id(0) == 0)
    def _():
        for c in range(chunks):
            for r in range(4):
                turned[r * part : (r + 1) * part, c * rows : (c + 1) * rows] = pieces[4 * c + r][...].T

    total = dot(turned[:, :rows], grads[0][...])
    for c in range(1, chunks):
        total += dot(turned[:, c * rows : (c + 1) * rows], grads[c][...])
    for r in range(4):
        at = pl.ds(pl.multiple_of(quarters[r] * part, part), part)
        out[at, :] = total[r * part : (r + 1) * part].astype(BF16)


def weights(quarters, pieces, grads, after):
    chunks = len(pieces)
    flat = [p for chunk in pieces for p in chunk]
    part = flat[0].shape[1]
    rows, columns = grads[0].shape
    total = rows * chunks
    block = 512

    def fixed(a):
        return pl.BlockSpec(a.shape, lambda c, n: (0, 0), pipeline_mode=pl.Buffered(1))

    return pl.pallas_call(
        functools.partial(weights_kernel, chunks=chunks),
        grid_spec=pltpu.PrefetchScalarGridSpec(
            num_scalar_prefetch=1,
            grid=(columns // block,),
            in_specs=[fixed(p) for p in flat]
            + [pl.BlockSpec((rows, block), lambda c, n: (0, c))] * chunks
            + [pl.BlockSpec(memory_space=pl.ANY)] * len(after),
            out_specs=pl.BlockSpec((4 * part, block), lambda c, n: (0, c)),
            scratch_shapes=[pltpu.VMEM((4 * part, total), BF16)],
        ),
        out_shape=jax.ShapeDtypeStruct((4 * part, columns), BF16),
        compiler_params=pltpu.CompilerParams(vmem_limit_bytes=60 * MIB),
        cost_estimate=pl.CostEstimate(
            flops=4 * 4 * part * total * columns, bytes_accessed=22_000_000, transcendentals=0
        ),
    )(quarters, *flat, *grads, *after)


def body(queries, slot_table, states, key_weight, value_weight, out_grad):
    devices = lax.axis_size("ctx")
    groups = lax.axis_size("tp")
    me = lax.axis_index("tp")
    stretches, neighbours = slot_table.shape
    slots, span, enc = states.shape
    capacity = 2
    places = devices * capacity
    part = enc // groups
    width = key_weight.shape[1]

    flat = slot_table.reshape(-1)
    live = flat >= 0
    owner = jnp.where(live, flat // slots, -1)
    count = flat.shape[0]
    order = jnp.arange(count)
    alike = (owner[:, None] == owner[None, :]) & (order[None, :] < order[:, None])
    rank = jnp.sum(alike.astype(jnp.int32), axis=1)
    place = jnp.where(live, owner * capacity + rank, -1)
    counts = jnp.sum(live.reshape(stretches, neighbours).astype(jnp.int32), axis=1)
    hit = place[:, None] == jnp.arange(places)[None, :]
    asked = jnp.sum(jnp.where(hit, (flat % slots + 1)[:, None], 0), axis=0) - 1
    source = jnp.sum(jnp.where(hit, order[:, None], 0), axis=0)
    wanted = lax.all_to_all(asked.reshape(devices, capacity), "ctx", 0, 0, tiled=True).reshape(-1)
    goes = wanted[None, :] == jnp.arange(slots)[:, None]
    landing = jnp.sum(jnp.where(goes, jnp.arange(places)[None, :], 0), axis=1)

    quarters = (me + jnp.array([0, groups - 1, 1, 2], jnp.int32)) % groups
    both = jnp.concatenate([key_weight, value_weight], axis=1)
    w = jnp.take(both.reshape(groups, part, 2 * width), quarters, axis=0, mode="clip")
    w = w.reshape(enc, 2 * width)
    wt = w.T

    mine = lax.dynamic_slice_in_dim(states, me * part, part, axis=2)
    picked = jnp.take(mine, jnp.maximum(wanted, 0), axis=0, mode="clip")
    arrived = lax.all_to_all(
        picked.reshape(devices, capacity, span, part), "ctx", 0, 0, tiled=True
    ).reshape(places, span, part)
    opening = jnp.repeat(place.reshape(stretches, neighbours)[:, :1], neighbours, axis=1)
    filled = jnp.where(live, place, opening.reshape(-1))

    def shift(by):
        return [(i, (i + by) % groups) for i in range(groups)]

    def permute(x, by):
        return lax.ppermute(x, "tp", shift(by))

    chunks = stretches // CHUNK
    here = CHUNK * neighbours
    owns = [
        jnp.take(arrived, filled[c * here : (c + 1) * here], axis=0, mode="clip").reshape(
            here * span, part
        )
        for c in range(chunks)
    ]

    def collect(own, after):
        if after:
            own, *_ = lax.optimization_barrier((own, *after))
        return [own, permute(own, 1), permute(own, -1), permute(own, 2)]

    pieces = [collect(owns[0], ())]
    after = ()
    done, summed = [], []
    got = ()
    for c in range(chunks):
        if c < chunks - 1:
            pieces.append(collect(owns[c + 1], pieces[-1][1:]))
        *tokens, p0, p1, p2, p3 = attend(
            counts, pieces[c], w, wt, queries, out_grad, after, c * CHUNK, CHUNK, span
        )
        done.append(tokens)
        p0, p1, p2, p3, *_ = lax.optimization_barrier((p0, p1, p2, p3, *pieces[-1][1:], *got))
        got = [p0, permute(p1, -1), permute(p2, 1), permute(p3, 2)]
        after = summed[-1:]
        total = sum(g.astype(F32) for g in got)
        summed.append(total.astype(BF16).reshape(here, span, part))
    attended, query_grad = (jnp.concatenate([t[i] for t in done], axis=0) for i in range(2))
    grads = [t[2] for t in done]

    terms = weights(quarters, pieces, grads, after)
    leaving = jnp.take(jnp.concatenate(summed, axis=0), source, axis=0, mode="clip")
    landed = lax.all_to_all(
        leaving.reshape(devices, capacity, span, part), "ctx", 0, 0, tiled=True
    ).reshape(places, span, part)
    states_grad = jnp.take(landed, landing, axis=0, mode="clip")
    terms, *_ = lax.optimization_barrier((terms, leaving))
    terms = lax.all_to_all(
        terms.reshape(devices, enc // devices, 2 * width), "ctx", 0, 0, tiled=True
    )
    weight_grads = jnp.sum(terms.astype(F32), axis=0)
    return (
        attended,
        query_grad,
        states_grad,
        weight_grads[:, :width],
        weight_grads[:, width:],
    )


def solution(mesh):
    in_specs = (
        P("ctx", "tp"),
        P("ctx", None),
        P("ctx", None, None),
        P(None, "tp"),
        P(None, "tp"),
        P("ctx", "tp"),
    )
    out_specs = (
        P("ctx", "tp"),
        P("ctx", "tp"),
        P("ctx", None, "tp"),
        P("ctx", "tp"),
        P("ctx", "tp"),
    )
    return jax.shard_map(body, mesh=mesh, in_specs=in_specs, out_specs=out_specs, check_vma=False)
```

time: 569 us -> 249 us (0.44)
  waiting for transfers between devices: 269 us -> 69.8 us
  matrix products: 102 us -> 0 us
  local copies, waits for them, and re-layouts: 102 us -> 29 us
  Pallas kernels: 0 us -> 63.5 us
  starting transfers between devices: 13.1 us -> 35 us
  other arithmetic: 35.2 us -> 13.8 us
  between operations: 14.4 us -> 0.89 us
  blocking collectives: 27.1 us -> 36.1 us
    reduce_scatter x2 -> x0, waiting for transfers between devices: 124 us -> none  [the longest x1 79 us: body(): lax.psum_scatter(value_terms.astype(jnp.bfloat16), 'ctx', scatter_dimensi...]
    dot_general x12 -> x0, matrix products: 102 us -> none  [the longest x1 10.8 us: body(): lax.dot_general(key_grad, key_weight, over_cols, preferred_element_type=j...]
    pallas_call x0 -> x3, Pallas kernels: none -> 63.5 us  [the longest x2 47.9 us: attend(): pl.pallas_call(functools.partial(attend_kernel, heads=heads, span=span, f...]
    all_to_all x2 -> x3, waiting for transfers between devices: 107 us -> 57.8 us  [the longest x1 28.3 us: body(): lax.all_to_all(picked.reshape(devices, capacity, span, part), 'ctx', 0, 0...]
    unnamed x38 -> x21, local copies, waits for them, and re-layouts: 45.6 us -> 1.72 us
    unnamed x4 -> x0, waiting for transfers between devices: 38.9 us -> none
    all_to_all x0 -> x1, blocking collectives: none -> 36.1 us  [body(): lax.all_to_all(terms.reshape(devices, enc // devices, 2 * width), 'ctx',...]
    all_gather x1 -> x0, blocking collectives: 27.1 us -> none  [body(): tables = lax.all_gather(slot_table, 'ctx', axis=0, tiled=True)]
  transfers between devices with their start and end apart: 5 -> 15, of which waited for: 4 -> 6; matrix products, arithmetic and copies ran while one was open for 9% -> 9% of each run, Pallas kernels for 0% -> 26%
where the time goes in v1:
time: 249 us; the launch traced here: 248 us
  waiting for transfers between devices  69.8 us (28%)
  Pallas kernels  63.5 us (26%)
  blocking collectives  36.1 us (14%)
  starting transfers between devices  35 us (14%)
  local copies, waits for them, and re-layouts  29 us (12%)
  other arithmetic  13.8 us (6%)
    pallas_call x2, Pallas kernels, attend(): pl.pallas_call(functools.partial(attend_kernel, heads=heads, span=span, f...  47.9 us
    all_to_all x1, blocking collectives, body(): lax.all_to_all(terms.reshape(devices, enc // devices, 2 * width), 'ctx',...  36.1 us
    all_to_all x1, waiting for transfers between devices, body(): lax.all_to_all(picked.reshape(devices, capacity, span, part), 'ctx', 0, 0...  28.3 us
    all_to_all x1, waiting for transfers between devices, body(): lax.all_to_all(leaving.reshape(devices, capacity, span, part), 'ctx', 0,...  23.7 us
    ppermute x12, starting transfers between devices, permute(): return lax.ppermute(x, 'tp', shift(by))  15.9 us
    pallas_call x1, Pallas kernels, weights(): pl.pallas_call(functools.partial(weights_kernel, chunks=chunks), grid_spe...  15.7 us
    ppermute x12, waiting for transfers between devices, permute(): return lax.ppermute(x, 'tp', shift(by))  12 us
    all_to_all x1, starting transfers between devices, body(): lax.all_to_all(asked.reshape(devices, capacity), 'ctx', 0, 0, tiled=True)  9.43 us
  transfers between devices with their start and end apart: 15, of which 6 were waited for; matrix products, arithmetic and copies ran while one was open for 9% of the time, Pallas kernels for 26%

profile of v1, /device:TPU:1, one launch (start us, length us, event | category | flops | bytes accessed | tf_op | source)
XLA Modules:
  0.0 248.1 jit_solution(18302058477385874949)
XLA Ops:
  3.9 9.4 %all-to-all-start = ((s32[32,1,2]{2,1,0:T(1,128)}), s32[32,1,2]{2,1,0:T(1,128)S(1)}, u32[]{:S(2)}, u32[]{:S(2)}) async-start(s32[32,1,2]{2,1,0:T(1,128)} %bitcast), calls=%async_computation | async-start | bytes 32768 | tf_op jit(solution)/shard_map/all_to_all | solution.py:180
  13.4 1.1 constant_dynamic-slice_fusion
  14.5 5.8 %all-to-all-done = s32[32,1,2]{2,1,0:T(1,128)S(1)} async-done(((s32[32,1,2]{2,1,0:T(1,128)}), s32[32,1,2]{2,1,0:T(1,128)S(1)}, u32[]{:S(2)}, u32[]{:S(2)}) %all-to-all-start) | async-done | bytes 288 | tf_op jit(solution)/shard_map/all_to_all | solution.py:180
  21.6 3.3 %gather_fusion = bf16[64,128,128]{2,1,0:T(8,128)(2,1)} fusion(bf16[26,128,128]{2,1,0:T(8,128)(2,1)} %constant_dynamic-slice_fusion, s32[1024]{0:T(1024)S(1)} %pad_clamp_fusion.5), kind=kCustom, calls=%fused_computation | custom fusion | bytes 4194560 | tf_op jit(solution)/shard_map/jit(_take)/gather | solution.py:191
  24.9 5.1 %all-to-all-start.1 = ((bf16[32,2,128,128]{3,2,1,0:T(8,128)(2,1)}), bf16[32,2,128,128]{3,2,1,0:T(8,128)(2,1)}, u32[]{:S(2)}, u32[]{:S(2)}) async-start(bf16[32,2,128,128]{3,2,1,0:T(8,128)(2,1)} %bitcast.19), calls=%async_computation.1 | async-start | bytes 4194304 | tf_op jit(solution)/shard_map/all_to_all | solution.py:192
  30.1 28.3 %all-to-all-done.1 = bf16[32,2,128,128]{3,2,1,0:T(8,128)(2,1)} async-done(((bf16[32,2,128,128]{3,2,1,0:T(8,128)(2,1)}), bf16[32,2,128,128]{3,2,1,0:T(8,128)(2,1)}, u32[]{:S(2)}, u32[]{:S(2)}) %all-to-all-start.1) | async-done | bytes 2097184 | tf_op jit(solution)/shard_map/all_to_all | solution.py:192
  58.5 3.0 %gather_fusion.1 = bf16[16,128,128]{2,1,0:T(8,128)(2,1)} fusion(bf16[64,128,128]{2,1,0:T(8,128)(2,1)} %bitcast.2, s32[1024]{0:T(1024)S(1)} %get-tuple-element.72), kind=kCustom, calls=%fused_computation.1 | custom fusion | bytes 1048640 | tf_op jit(solution)/shard_map/jit(_take)/gather | solution.py:207
  61.5 2.9 %collective-permute-start.2 = (bf16[2048,128]{1,0:T(8,128)(2,1)}, bf16[2048,128]{1,0:T(8,128)(2,1)}, u32[]{:S(2)}, u32[]{:S(2)}) collective-permute-start(bf16[2048,128]{1,0:T(8,128)(2,1)} %bitcast.27), channel_id=1, source_target_pairs={{0,2},{1,3},{2,0},{3,1},{4,6},{5,7},{6,4},{7,5},{8,10},{9,11},{10,... | collective-permute-start | bytes 1572872 | tf_op jit(solution)/shard_map/ppermute | solution.py:202
  65.9 3.1 %pad_maximum_fusion = bf16[512,2048]{1,0:T(8,128)(2,1)} fusion(bf16[512,1024]{1,0:T(8,128)(2,1)} %param.11, bf16[512,1024]{1,0:T(8,128)(2,1)} %param.10), kind=kLoop, calls=%fused_computation.7 | loop fusion | flops 4194304 | bytes 4194304 | tf_op jit(solution)/shard_map/concatenate | solution.py:185
  69.0 3.6 %gather_fusion.2 = bf16[4,128,2048]{2,1,0:T(8,128)(2,1)} fusion(bf16[4,128,2048]{2,1,0:T(8,128)(2,1)} %bitcast.20, s32[1024]{0:T(1024)S(1)} %pad_clamp_fusion.3), kind=kCustom, calls=%fused_computation.2 | custom fusion | bytes 4194320 | tf_op jit(solution)/shard_map/jit(_take)/gather | solution.py:186
  72.6 3.9 %copy.41 = bf16[512,2048]{0,1:T(8,128)(2,1)} copy(bf16[512,2048]{1,0:T(8,128)(2,1)} %bitcast.15) | data formatting | bytes 4194304 | tf_op jit(solution)/shard_map/reshape | solution.py:187
  76.5 3.0 %gather_fusion.3 = bf16[16,128,128]{2,1,0:T(8,128)(2,1)} fusion(bf16[64,128,128]{2,1,0:T(8,128)(2,1)} %bitcast.2, s32[1024]{0:T(1024)S(1)} %get-tuple-element.71), kind=kCustom, calls=%fused_computation.3 | custom fusion | bytes 1048640 | tf_op jit(solution)/shard_map/jit(_take)/gather | solution.py:207
  79.5 8.2 %collective-permute-done.1.s2.refs_2_ = bf16[2048,128]{1,0:T(8,128)(2,1)} collective-permute-done((bf16[2048,128]{1,0:T(8,128)(2,1)}, bf16[2048,128]{1,0:T(8,128)(2,1)}, u32[]{:S(2)}, u32[]{:S(2)}) %collective-permute-start.1) | collective-permute-done | bytes 524320 | tf_op jit(solution)/shard_map/ppermute | solution.py:202
  88.4 2.9 %collective-permute-start.5 = (bf16[2048,128]{1,0:T(8,128)(2,1)}, bf16[2048,128]{1,0:T(8,128)(2,1)S(1)}, u32[]{:S(2)}, u32[]{:S(2)}) collective-permute-start(bf16[2048,128]{1,0:T(8,128)(2,1)} %bitcast.32), channel_id=1, source_target_pairs={{0,2},{1,3},{2,0},{3,1},{4,6},{5,7},{6,4},{7,5},{8,10},{9,11},{10,... | collective-permute-start | bytes 1572872 | tf_op jit(solution)/shard_map/ppermute | solution.py:202
  92.8 23.9 %shard_map.110 = (bf16[256,1024]{1,0:T(8,128)(2,1)}, bf16[256,1024]{1,0:T(8,128)(2,1)}, bf16[2048,2048]{1,0:T(8,128)(2,1)}, bf16[2048,128]{1,0:T(8,128)(2,1)}, b...) custom-call(s32[8]{0:T(128)} %get-tuple-element.65.counts, ...), custom_call_target="tpu_custom_call" | custom-call | flops 24000000000 | bytes 4000000 | tf_op jit(solution)/shard_map/pallas_call | solution.py:88
  117.5 2.0 collective-permute-start.6
  119.5 1.2 collective-permute-start.8
  120.7 23.9 %shard_map.111 = (bf16[256,1024]{1,0:T(8,128)(2,1)}, bf16[256,1024]{1,0:T(8,128)(2,1)}, bf16[2048,2048]{1,0:T(8,128)(2,1)}, bf16[2048,128]{1,0:T(8,128)(2,1)}, b...) custom-call(s32[8]{0:T(128)} %get-tuple-element.65.counts, ...), custom_call_target="tpu_custom_call" | custom-call | flops 24000000000 | bytes 4000000 | tf_op jit(solution)/shard_map/pallas_call | solution.py:88
  144.7 1.6 collective-permute-start.9
  146.9 1.7 collective-permute-start.11
  148.6 2.4 add_convert_fusion.1
  151.0 15.7 %shard_map.112 = bf16[512,2048]{1,0:T(8,128)(2,1)} custom-call(s32[4]{0:T(128)} %copy-done.7, bf16[2048,128]{1,0:T(8,128)(2,1)} %bitcast.31, bf16[2048,128]{1,0:T(8,128)(2,1)} %collective-permute-done.s1.refs_1_, bf16[2048,128]{1,0:T(8,128)(2,1)} %collective-permute-done.1.s2.refs_2_, bf16[2048,128]{1,0:T(8,128)(2,1)} %collective-permute-done.2.s3.refs_3_, ...), custom_call_target="tpu_custom_call" | custom-call | flops 17179869184 | bytes 22000000 | tf_op jit(solution)/shard_map/pallas_call | solution.py:138
  166.7 3.1 %collective-permute-done.11 = bf16[2048,128]{1,0:T(8,128)(2,1)} collective-permute-done((bf16[2048,128]{1,0:T(8,128)(2,1)}, bf16[2048,128]{1,0:T(8,128)(2,1)}, u32[]{:S(2)}, u32[]{:S(2)}) %collective-permute-start.11) | collective-permute-done | bytes 524320 | tf_op jit(solution)/shard_map/ppermute | solution.py:202
  169.8 1.6 add_convert_fusion
  171.4 1.1 pad_maximum_fusion.3
  172.5 3.4 %gather_fusion.4 = bf16[64,128,128]{2,1,0:T(8,128)(2,1)} fusion(bf16[32,128,128]{2,1,0:T(8,128)(2,1)} %pad_maximum_fusion.3, s32[1024]{0:T(1024)S(1)} %pad_clamp_fusion.1), kind=kCustom, calls=%fused_computation.4 | custom fusion | bytes 4194560 | tf_op jit(solution)/shard_map/jit(_take)/gather | solution.py:238
  175.9 36.1 %all_to_all.21 = bf16[32,16,2048]{2,1,0:T(8,128)(2,1)} all-to-all(bf16[32,16,2048]{2,1,0:T(8,128)(2,1)} %bitcast.23), channel_id=1, replica_groups=mesh['ctx'=32,'tp'=4] {'ctx'}, dimensions={0} | all-to-all | bytes 4194304 | tf_op jit(solution)/shard_map/all_to_all | solution.py:244
  212.0 4.5 %all-to-all-start.2 = ((bf16[32,2,128,128]{3,2,1,0:T(8,128)(2,1)}), bf16[32,2,128,128]{3,2,1,0:T(8,128)(2,1)}, u32[]{:S(2)}, u32[]{:S(2)}) async-start(bf16[32,2,128,128]{3,2,1,0:T(8,128)(2,1)} %bitcast.18), calls=%async_computation.2 | async-start | bytes 4194304 | tf_op jit(solution)/shard_map/all_to_all | solution.py:239
  216.8 2.4 pad_maximum_fusion.1
  219.2 1.0 pad_maximum_fusion.2
  221.3 23.7 %all-to-all-done.2 = bf16[32,2,128,128]{3,2,1,0:T(8,128)(2,1)} async-done(((bf16[32,2,128,128]{3,2,1,0:T(8,128)(2,1)}), bf16[32,2,128,128]{3,2,1,0:T(8,128)(2,1)}, u32[]{:S(2)}, u32[]{:S(2)}) %all-to-all-start.2) | async-done | bytes 2097184 | tf_op jit(solution)/shard_map/all_to_all | solution.py:239
  244.9 3.2 %gather_fusion.5 = bf16[26,128,128]{2,1,0:T(8,128)(2,1)} fusion(bf16[64,128,128]{2,1,0:T(8,128)(2,1)} %bitcast.11, s32[1024]{0:T(1024)S(1)} %pad_clamp_fusion), kind=kCustom, calls=%fused_computation.5 | custom fusion | bytes 1704040 | tf_op jit(solution)/shard_map/jit(_take)/gather | solution.py:242
  (68 shorter events, 11.0 us)
Async XLA Ops:
  0.6 12.8 %copy-start = (bf16[26,128,512]{2,1,0:T(8,128)(2,1)S(1)}, bf16[26,128,512]{2,1,0:T(8,128)(2,1)}, u32[]{:S(2)}) copy-start(bf16[26,128,512]{2,1,0:T(8,128)(2,1)} %param.9) | copy-start | bytes 10223620
  3.9 16.3 %all-to-all-start = ((s32[32,1,2]{2,1,0:T(1,128)}), s32[32,1,2]{2,1,0:T(1,128)S(1)}, u32[]{:S(2)}, u32[]{:S(2)}) async-start(s32[32,1,2]{2,1,0:T(1,128)} %bitcast), calls=%async_computation | async-start | bytes 32768 | tf_op jit(solution)/shard_map/all_to_all | solution.py:180
  24.9 41.0 %copy-start.9 = (s32[4]{0:T(128)S(1)}, s32[4]{0:T(128)}, u32[]{:S(2)}) copy-start(s32[4]{0:T(128)} %constant.55.clone) | copy-start | bytes 52
  24.9 33.6 %all-to-all-start.1 = ((bf16[32,2,128,128]{3,2,1,0:T(8,128)(2,1)}), bf16[32,2,128,128]{3,2,1,0:T(8,128)(2,1)}, u32[]{:S(2)}, u32[]{:S(2)}) async-start(bf16[32,2,128,128]{3,2,1,0:T(8,128)(2,1)} %bitcast.19), calls=%async_computation.1 | async-start | bytes 4194304 | tf_op jit(solution)/shard_map/all_to_all | solution.py:192
  61.5 18.0 %collective-permute-start.2 = (bf16[2048,128]{1,0:T(8,128)(2,1)}, bf16[2048,128]{1,0:T(8,128)(2,1)}, u32[]{:S(2)}, u32[]{:S(2)}) collective-permute-start(bf16[2048,128]{1,0:T(8,128)(2,1)} %bitcast.27), channel_id=1, source_target_pairs={{0,2},{1,3},{2,0},{3,1},{4,6},{5,7},{6,4},{7,5},{8,10},{9,11},{10,... | collective-permute-start | bytes 1572872 | tf_op jit(solution)/shard_map/ppermute | solution.py:202
  64.4 23.3 %collective-permute-start.1 = (bf16[2048,128]{1,0:T(8,128)(2,1)}, bf16[2048,128]{1,0:T(8,128)(2,1)}, u32[]{:S(2)}, u32[]{:S(2)}) collective-permute-start(bf16[2048,128]{1,0:T(8,128)(2,1)} %bitcast.28), channel_id=1, source_target_pairs={{0,3},{1,0},{2,1},{3,2},{4,7},{5,4},{6,5},{7,6},{8,11},{9,8},{10,9... | collective-permute-start | bytes 1572872 | tf_op jit(solution)/shard_map/ppermute | solution.py:202
  65.2 23.2 %collective-permute-start = (bf16[2048,128]{1,0:T(8,128)(2,1)}, bf16[2048,128]{1,0:T(8,128)(2,1)}, u32[]{:S(2)}, u32[]{:S(2)}) collective-permute-start(bf16[2048,128]{1,0:T(8,128)(2,1)} %bitcast.29), channel_id=1, source_target_pairs={{0,1},{1,2},{2,3},{3,0},{4,5},{5,6},{6,7},{7,4},{8,9},{9,10},{10,1... | collective-permute-start | bytes 1572872 | tf_op jit(solution)/shard_map/ppermute | solution.py:202
  65.9 3.1 %copy-start.7 = (s32[4]{0:T(128)}, s32[4]{0:T(128)S(1)}, u32[]{:S(2)}) copy-start(s32[4]{0:T(128)S(1)} %and_select_fusion.quarters) | copy-start | bytes 52
  88.4 28.3 %collective-permute-start.5 = (bf16[2048,128]{1,0:T(8,128)(2,1)}, bf16[2048,128]{1,0:T(8,128)(2,1)S(1)}, u32[]{:S(2)}, u32[]{:S(2)}) collective-permute-start(bf16[2048,128]{1,0:T(8,128)(2,1)} %bitcast.32), channel_id=1, source_target_pairs={{0,2},{1,3},{2,0},{3,1},{4,6},{5,7},{6,4},{7,5},{8,10},{9,11},{10,... | collective-permute-start | bytes 1572872 | tf_op jit(solution)/shard_map/ppermute | solution.py:202
  91.3 25.4 %collective-permute-start.4 = (bf16[2048,128]{1,0:T(8,128)(2,1)}, bf16[2048,128]{1,0:T(8,128)(2,1)}, u32[]{:S(2)}, u32[]{:S(2)}) collective-permute-start(bf16[2048,128]{1,0:T(8,128)(2,1)} %bitcast.33), channel_id=1, source_target_pairs={{0,3},{1,0},{2,1},{3,2},{4,7},{5,4},{6,5},{7,6},{8,11},{9,8},{10,9... | collective-permute-start | bytes 1572872 | tf_op jit(solution)/shard_map/ppermute | solution.py:202
  92.1 24.7 %collective-permute-start.3 = (bf16[2048,128]{1,0:T(8,128)(2,1)}, bf16[2048,128]{1,0:T(8,128)(2,1)}, u32[]{:S(2)}, u32[]{:S(2)}) collective-permute-start(bf16[2048,128]{1,0:T(8,128)(2,1)} %bitcast.34), channel_id=1, source_target_pairs={{0,1},{1,2},{2,3},{3,0},{4,5},{5,6},{6,7},{7,4},{8,9},{9,10},{10,1... | collective-permute-start | bytes 1572872 | tf_op jit(solution)/shard_map/ppermute | solution.py:202
  116.7 0.8 copy-start.8
  117.5 31.1 %copy-start.3 = (bf16[2048,128]{1,0:T(8,128)(2,1)S(1)}, bf16[2048,128]{1,0:T(8,128)(2,1)}, u32[]{:S(2)}) copy-start(bf16[2048,128]{1,0:T(8,128)(2,1)} %get-tuple-element.38) | copy-start | bytes 1572868
  117.5 27.1 %collective-permute-start.6 = (bf16[2048,128]{1,0:T(8,128)(2,1)}, bf16[2048,128]{1,0:T(8,128)(2,1)}, u32[]{:S(2)}, u32[]{:S(2)}) collective-permute-start(bf16[2048,128]{1,0:T(8,128)(2,1)} %get-tuple-element.39), channel_id=1, source_target_pairs={{0,3},{1,0},{2,1},{3,2},{4,7},{5,4},{6,5},{7,6},{8,11},{9,8},{10,9... | collective-permute-start | bytes 1572872 | tf_op jit(solution)/shard_map/ppermute | solution.py:202
  119.5 25.1 %collective-permute-start.7 = (bf16[2048,128]{1,0:T(8,128)(2,1)}, bf16[2048,128]{1,0:T(8,128)(2,1)}, u32[]{:S(2)}, u32[]{:S(2)}) collective-permute-start(bf16[2048,128]{1,0:T(8,128)(2,1)} %get-tuple-element.40), channel_id=1, source_target_pairs={{0,1},{1,2},{2,3},{3,0},{4,5},{5,6},{6,7},{7,4},{8,9},{9,10},{10,1... | collective-permute-start | bytes 1572872 | tf_op jit(solution)/shard_map/ppermute | solution.py:202
  119.5 25.1 %collective-permute-start.8 = (bf16[2048,128]{1,0:T(8,128)(2,1)}, bf16[2048,128]{1,0:T(8,128)(2,1)}, u32[]{:S(2)}, u32[]{:S(2)}) collective-permute-start(bf16[2048,128]{1,0:T(8,128)(2,1)} %get-tuple-element.41), channel_id=1, source_target_pairs={{0,2},{1,3},{2,0},{3,1},{4,6},{5,7},{6,4},{7,5},{8,10},{9,11},{10,... | collective-permute-start | bytes 1572872 | tf_op jit(solution)/shard_map/ppermute | solution.py:202
  144.7 22.0 %collective-permute-start.9 = (bf16[2048,128]{1,0:T(8,128)(2,1)}, bf16[2048,128]{1,0:T(8,128)(2,1)}, u32[]{:S(2)}, u32[]{:S(2)}) collective-permute-start(bf16[2048,128]{1,0:T(8,128)(2,1)} %get-tuple-element.47), channel_id=1, source_target_pairs={{0,3},{1,0},{2,1},{3,2},{4,7},{5,4},{6,5},{7,6},{8,11},{9,8},{10,9... | collective-permute-start | bytes 1572872 | tf_op jit(solution)/shard_map/ppermute | solution.py:202
  146.2 20.5 %collective-permute-start.10 = (bf16[2048,128]{1,0:T(8,128)(2,1)}, bf16[2048,128]{1,0:T(8,128)(2,1)}, u32[]{:S(2)}, u32[]{:S(2)}) collective-permute-start(bf16[2048,128]{1,0:T(8,128)(2,1)} %get-tuple-element.48), channel_id=1, source_target_pairs={{0,1},{1,2},{2,3},{3,0},{4,5},{5,6},{6,7},{7,4},{8,9},{9,10},{10,1... | collective-permute-start | bytes 1572872 | tf_op jit(solution)/shard_map/ppermute | solution.py:202
  146.9 22.9 %collective-permute-start.11 = (bf16[2048,128]{1,0:T(8,128)(2,1)}, bf16[2048,128]{1,0:T(8,128)(2,1)}, u32[]{:S(2)}, u32[]{:S(2)}) collective-permute-start(bf16[2048,128]{1,0:T(8,128)(2,1)} %get-tuple-element.49), channel_id=1, source_target_pairs={{0,2},{1,3},{2,0},{3,1},{4,6},{5,7},{6,4},{7,5},{8,10},{9,11},{10,... | collective-permute-start | bytes 1572872 | tf_op jit(solution)/shard_map/ppermute | solution.py:202
  151.0 18.8 %copy-start.4 = (bf16[2048,128]{1,0:T(8,128)(2,1)S(1)}, bf16[2048,128]{1,0:T(8,128)(2,1)}, u32[]{:S(2)}) copy-start(bf16[2048,128]{1,0:T(8,128)(2,1)} %get-tuple-element.46) | copy-start | bytes 1572868
  166.7 4.7 %copy-start.2 = (bf16[2048,128]{1,0:T(8,128)(2,1)S(1)}, bf16[2048,128]{1,0:T(8,128)(2,1)}, u32[]{:S(2)}) copy-start(bf16[2048,128]{1,0:T(8,128)(2,1)} %add_convert_fusion.1) | copy-start | bytes 1572868
  212.0 32.9 %all-to-all-start.2 = ((bf16[32,2,128,128]{3,2,1,0:T(8,128)(2,1)}), bf16[32,2,128,128]{3,2,1,0:T(8,128)(2,1)}, u32[]{:S(2)}, u32[]{:S(2)}) async-start(bf16[32,2,128,128]{3,2,1,0:T(8,128)(2,1)} %bitcast.18), calls=%async_computation.2 | async-start | bytes 4194304 | tf_op jit(solution)/shard_map/all_to_all | solution.py:239
  216.7 2.5 %copy-start.5 = (bf16[256,1024]{1,0:T(8,128)(2,1)S(1)}, bf16[256,1024]{1,0:T(8,128)(2,1)}, u32[]{:S(2)}) copy-start(bf16[256,1024]{1,0:T(8,128)(2,1)} %get-tuple-element.32) | copy-start | bytes 1572868
  216.7 2.5 %copy-start.6 = (bf16[256,1024]{1,0:T(8,128)(2,1)S(1)}, bf16[256,1024]{1,0:T(8,128)(2,1)}, u32[]{:S(2)}) copy-start(bf16[256,1024]{1,0:T(8,128)(2,1)} %get-tuple-element.33) | copy-start | bytes 1572868
  216.8 3.4 %copy-start.1 = (bf16[32,16,2048]{2,1,0:T(8,128)(2,1)S(1)}, bf16[32,16,2048]{2,1,0:T(8,128)(2,1)}, u32[]{:S(2)}) copy-start(bf16[32,16,2048]{2,1,0:T(8,128)(2,1)} %all_to_all.21) | copy-start | bytes 6291460

commit v2 on v1

--- a/solution.py
+++ b/solution.py
@@ -21,8 +21,10 @@
     return lax.dot_general(a, b, dims, preferred_element_type=F32)
 
 
-def attend_kernel(counts, s0, s1, s2, s3, w, wt, q_ref, do_ref, *rest, heads, span, first):
-    att, qg, grads, p0, p1, p2, p3, kv = rest[-8:]
+def attend_kernel(
+    counts, quarters, s0, s1, s2, s3, w, wt, q_ref, do_ref, *rest, heads, span, first, before, last
+):
+    att, qg, p0, p1, p2, p3, out, kv, grads, total = rest[-10:]
     c = pl.program_id(0)
     width = heads * HEAD_DIM
     scale = HEAD_DIM ** (-0.5)
@@ -60,6 +62,19 @@
         both = (dot(dscores_b, k, TN) * scale).astype(BF16)
         qg[:, lo:mid] = both[:length, :HEAD_DIM]
         qg[:, mid:hi] = both[length:, HEAD_DIM:]
+    terms = dot(states, grads[...], TN)
+    if before:
+        total[...] = jnp.where(c == 0, rest[0][...], total[...]) + terms
+    else:
+
+        @pl.when(c == 0)
+        def _():
+            total[...] = terms
+
+        @pl.when(c > 0)
+        def _():
+            total[...] += terms
+
     part = dot(grads[...], wt[...]).astype(BF16)
     n = p0.shape[1]
     p0[...] = part[:, :n]
@@ -67,91 +82,88 @@
     p2[...] = part[:, 2 * n : 3 * n]
     p3[...] = part[:, 3 * n :]
 
-
-def attend(counts, pieces, w, wt, q, do, after, first, number, span):
+    @pl.when(c == pl.num_programs(0) - 1)
+    def _():
+        if not last:
+            out[...] = total[...]
+            return
+        for r in range(4):
+            at = pl.ds(pl.multiple_of(quarters[r] * n, n), n)
+            out[at, :] = total[r * n : (r + 1) * n, :].astype(BF16)
+
+
+def attend(counts, quarters, pieces, w, wt, q, do, terms, after, first, number, span):
     heads = q.shape[1] // HEAD_DIM
     stretches = counts.shape[0]
     length = q.shape[0] // stretches
     width = q.shape[1]
     rows = pieces[0].shape[0] // number
     part = pieces[0].shape[1]
-    piece = pl.BlockSpec((rows, part), lambda c, n: (c, 0))
-    token = pl.BlockSpec((length, width), lambda c, n: (first + c, 0))
-    whole = pl.BlockSpec((rows, 2 * width), lambda c, n: (c, 0))
-    token_out = pl.BlockSpec((length, width), lambda c, n: (c, 0))
+    last = first + number == stretches
+    piece = pl.BlockSpec((rows, part), lambda c, *_: (c, 0))
+    token = pl.BlockSpec((length, width), lambda c, *_: (first + c, 0))
+    token_out = pl.BlockSpec((length, width), lambda c, *_: (c, 0))
     anywhere = pl.BlockSpec(memory_space=pl.ANY)
 
     def fixed(a):
-        return pl.BlockSpec(a.shape, lambda c, n: (0, 0), pipeline_mode=pl.Buffered(1))
+        return pl.BlockSpec(a.shape, lambda c, *_: (0, 0), pipeline_mode=pl.Buffered(1))
 
     shape = jax.ShapeDtypeStruct
+    sums = shape(w.shape, BF16 if last else F32)
     return pl.pallas_call(
-        functools.partial(attend_kernel, heads=heads, span=span, first=first),
+        functools.partial(
+            attend_kernel, heads=heads, span=span, first=first, before=bool(terms), last=last
+        ),
         grid_spec=pltpu.PrefetchScalarGridSpec(
-            num_scalar_prefetch=1,
+            num_scalar_prefetch=2,
             grid=(number,),
-            in_specs=[piece] * 4 + [fixed(w), fixed(wt), token, token] + [anywhere] * len(after),
-            out_specs=[token_out, token_out, whole] + [piece] * 4,
-            scratch_shapes=[pltpu.VMEM((rows, 2 * width), BF16)],
+            in_specs=[piece] * 4
+            + [fixed(w), fixed(wt), token, token]
+            + [fixed(t) for t in terms]
+            + [anywhere] * len(after),
+            out_specs=[token_out, token_out] + [piece] * 4 + [fixed(sums)],
+            scratch_shapes=[
+                pltpu.VMEM((rows, 2 * width), BF16),
+                pltpu.VMEM((rows, 2 * width), BF16),
+                pltpu.VMEM(w.shape, F32),
+            ],
         ),
         out_shape=[shape((number * length, width), BF16)] * 2
-        + [shape((number * rows, 2 * width), BF16)]
-        + [shape((number * rows, part), BF16)] * 4,
+        + [shape((number * rows, part), BF16)] * 4
+        + [sums],
         compiler_params=pltpu.CompilerParams(vmem_limit_bytes=60 * MIB),
         cost_estimate=pl.CostEstimate(
             flops=number * 6_000_000_000, bytes_accessed=4_000_000, transcendentals=0
         ),
-    )(counts, *pieces, w, wt, q, do, *after)
-
-
-def weights_kernel(quarters, *refs, chunks):
-    pieces, grads = refs[: 4 * chunks], refs[4 * chunks : 5 * chunks]
-    out, turned = refs[-2:]
-    part = pieces[0].shape[1]
-    rows = pieces[0].shape[0]
-
-    @pl.when(pl.program_id(0) == 0)
-    def _():
-        for c in range(chunks):
-            for r in range(4):
-                turned[r * part : (r + 1) * part, c * rows : (c + 1) * rows] = pieces[4 * c + r][...].T
-
-    total = dot(turned[:, :rows], grads[0][...])
-    for c in range(1, chunks):
-        total += dot(turned[:, c * rows : (c + 1) * rows], grads[c][...])
-    for r in range(4):
-        at = pl.ds(pl.multiple_of(quarters[r] * part, part), part)
-        out[at, :] = total[r * part : (r + 1) * part].astype(BF16)
-
-
-def weights(quarters, pieces, grads, after):
-    chunks = len(pieces)
-    flat = [p for chunk in pieces for p in chunk]
-    part = flat[0].shape[1]
-    rows, columns = grads[0].shape
-    total = rows * chunks
-    block = 512
-
-    def fixed(a):
-        return pl.BlockSpec(a.shape, lambda c, n: (0, 0), pipeline_mode=pl.Buffered(1))
-
+    )(counts, quarters, *pieces, w, wt, q, do, *terms, *after)
+
+
+def merge_kernel(at, earlier, a, b, c, d, out, total):
+    half = earlier.shape[0]
+    total[:half] = earlier[...]
+    whole = a[...].astype(F32) + b[...].astype(F32) + (c[...].astype(F32) + d[...].astype(F32))
+    total[half:] = whole.astype(BF16).reshape(earlier.shape)
+    for i in range(out.shape[0]):
+        out[i] = total[at[i]]
+
+
+def merge(at, earlier, last):
+    half, span, part = earlier.shape
+    shape = at.shape + (span, part)
+    flat = pl.BlockSpec((half * span, part), lambda i, at: (0, 0))
     return pl.pallas_call(
-        functools.partial(weights_kernel, chunks=chunks),
+        merge_kernel,
         grid_spec=pltpu.PrefetchScalarGridSpec(
             num_scalar_prefetch=1,
-            grid=(columns // block,),
-            in_specs=[fixed(p) for p in flat]
-            + [pl.BlockSpec((rows, block), lambda c, n: (0, c))] * chunks
-            + [pl.BlockSpec(memory_space=pl.ANY)] * len(after),
-            out_specs=pl.BlockSpec((4 * part, block), lambda c, n: (0, c)),
-            scratch_shapes=[pltpu.VMEM((4 * part, total), BF16)],
-        ),
-        out_shape=jax.ShapeDtypeStruct((4 * part, columns), BF16),
-        compiler_params=pltpu.CompilerParams(vmem_limit_bytes=60 * MIB),
-        cost_estimate=pl.CostEstimate(
-            flops=4 * 4 * part * total * columns, bytes_accessed=22_000_000, transcendentals=0
-        ),
-    )(quarters, *flat, *grads, *after)
+            grid=(1,),
+            in_specs=[pl.BlockSpec(earlier.shape, lambda i, at: (0, 0, 0))] + [flat] * 4,
+            out_specs=pl.BlockSpec(shape, lambda i, at: (0, 0, 0)),
+            scratch_shapes=[pltpu.VMEM((2 * half, span, part), BF16)],
+        ),
+        out_shape=jax.ShapeDtypeStruct(shape, BF16),
+        compiler_params=pltpu.CompilerParams(vmem_limit_bytes=24 * MIB),
+        cost_estimate=pl.CostEstimate(flops=0, bytes_accessed=4_000_000, transcendentals=0),
+    )(at, earlier, *last)
 
 
 def body(queries, slot_table, states, key_weight, value_weight, out_grad):
@@ -216,35 +228,44 @@
         return [own, permute(own, 1), permute(own, -1), permute(own, 2)]
 
     pieces = [collect(owns[0], ())]
-    after = ()
+    after, terms, got = (), (), ()
     done, summed = [], []
-    got = ()
     for c in range(chunks):
         if c < chunks - 1:
             pieces.append(collect(owns[c + 1], pieces[-1][1:]))
-        *tokens, p0, p1, p2, p3 = attend(
-            counts, pieces[c], w, wt, queries, out_grad, after, c * CHUNK, CHUNK, span
+        *tokens, p0, p1, p2, p3, sums = attend(
+            counts, quarters, pieces[c], w, wt, queries, out_grad, terms, after, c * CHUNK, CHUNK, span
         )
         done.append(tokens)
-        p0, p1, p2, p3, *_ = lax.optimization_barrier((p0, p1, p2, p3, *pieces[-1][1:], *got))
-        got = [p0, permute(p1, -1), permute(p2, 1), permute(p3, 2)]
+        terms = (sums,)
+        p0, p1, p2, p3, sums, *_ = lax.optimization_barrier(
+            (p0, p1, p2, p3, sums, *pieces[-1][1:], *got)
+        )
+        far = permute(p3, 2)
+        if c == chunks - 1:
+            core = lax.axis_index("ctx") % 2
+            shares = sums.reshape(devices // 2, 2, enc // devices, 2 * width)
+            keep = lax.dynamic_index_in_dim(shares, core, 1, keepdims=False)
+            send = lax.dynamic_index_in_dim(shares, 1 - core, 1, keepdims=False)
+            found = lax.ppermute(send, "ctx", [(i, i ^ 1) for i in range(devices)])
+            chip = (keep.astype(F32) + found.astype(F32)).astype(BF16)
+            p1, p2, chip, far = lax.optimization_barrier((p1, p2, chip, far))
+        got = [p0, permute(p1, -1), permute(p2, 1), far]
         after = summed[-1:]
-        total = sum(g.astype(F32) for g in got)
-        summed.append(total.astype(BF16).reshape(here, span, part))
+        if c < chunks - 1:
+            total = sum(g.astype(F32) for g in got)
+            summed.append(total.astype(BF16).reshape(here, span, part))
     attended, query_grad = (jnp.concatenate([t[i] for t in done], axis=0) for i in range(2))
-    grads = [t[2] for t in done]
-
-    terms = weights(quarters, pieces, grads, after)
-    leaving = jnp.take(jnp.concatenate(summed, axis=0), source, axis=0, mode="clip")
+
+    same = [list(range(c, devices, 2)) for c in range(2)]
+    chip = lax.all_to_all(chip, "ctx", 0, 0, axis_index_groups=same, tiled=True)
+    weight_grads = jnp.sum(chip.astype(F32), axis=0)
+
+    leaving = merge(source, jnp.concatenate(summed, axis=0), got)
     landed = lax.all_to_all(
         leaving.reshape(devices, capacity, span, part), "ctx", 0, 0, tiled=True
     ).reshape(places, span, part)
     states_grad = jnp.take(landed, landing, axis=0, mode="clip")
-    terms, *_ = lax.optimization_barrier((terms, leaving))
-    terms = lax.all_to_all(
-        terms.reshape(devices, enc // devices, 2 * width), "ctx", 0, 0, tiled=True
-    )
-    weight_grads = jnp.sum(terms.astype(F32), axis=0)
     return (
         attended,
         query_grad,

time: 249 us -> 242 us (0.972)
  blocking collectives: 36.1 us -> 0 us
  waiting for transfers between devices: 69.8 us -> 88.3 us
  starting transfers between devices: 35 us -> 45.7 us
    all_to_all x1 -> x0, blocking collectives: 36.1 us -> none  [body(): lax.all_to_all(terms.reshape(devices, enc // devices, 2 * width), 'ctx',...]
    ppermute x12, waiting for transfers between devices: 12 us -> 30.6 us  [permute(): return lax.ppermute(x, 'tp', shift(by))]
    pallas_call x2, Pallas kernels: 47.9 us -> 61.4 us  [attend(): pl.pallas_call(functools.partial(attend_kernel, heads=heads, span=span, f...]
    pallas_call x1, Pallas kernels: 15.7 us -> 2.26 us  [merge(): pl.pallas_call(merge_kernel, grid_spec=pltpu.PrefetchScalarGridSpec(num_s...]
    all_to_all x0 -> x1, starting transfers between devices: none -> 4.34 us  [body(): chip = lax.all_to_all(chip, 'ctx', 0, 0, axis_index_groups=same, tiled=True)]
    all_to_all x1, starting transfers between devices: 4.55 us -> 8.57 us  [body(): lax.all_to_all(leaving.reshape(devices, capacity, span, part), 'ctx', 0,...]
    gather x1 -> x0, local copies, waits for them, and re-layouts: 3.37 us -> none  [body(): jnp.take(jnp.concatenate(summed, axis=0), source, axis=0, mode='clip')]
    convert_element_type x0 -> x1, other arithmetic: none -> 2.91 us  [body(): chip = (keep.astype(F32) + found.astype(F32)).astype(BF16)]
  transfers between devices with their start and end apart: 15 -> 17, of which waited for: 6 -> 9; matrix products, arithmetic and copies ran while one was open for 9% -> 10% of each run, Pallas kernels for 26% -> 26%
where the time goes in v2:
time: 242 us; the launch traced here: 241 us
  waiting for transfers between devices  88.3 us (36%)
  Pallas kernels  63.6 us (26%)
  starting transfers between devices  45.7 us (19%)
  local copies, waits for them, and re-layouts  28.5 us (12%)
  other arithmetic  14.3 us (6%)
    pallas_call x2, Pallas kernels, attend(): pl.pallas_call(functools.partial(attend_kernel, heads=heads, span=span, f...  61.4 us
    ppermute x12, waiting for transfers between devices, permute(): return lax.ppermute(x, 'tp', shift(by))  30.6 us
    all_to_all x1, waiting for transfers between devices, body(): lax.all_to_all(picked.reshape(devices, capacity, span, part), 'ctx', 0, 0...  28.3 us
    all_to_all x1, waiting for transfers between devices, body(): lax.all_to_all(leaving.reshape(devices, capacity, span, part), 'ctx', 0,...  22.7 us
    ppermute x12, starting transfers between devices, permute(): return lax.ppermute(x, 'tp', shift(by))  16.2 us
    all_to_all x1, starting transfers between devices, body(): lax.all_to_all(asked.reshape(devices, capacity), 'ctx', 0, 0, tiled=True)  9.43 us
    all_to_all x1, starting transfers between devices, body(): lax.all_to_all(leaving.reshape(devices, capacity, span, part), 'ctx', 0,...  8.57 us
    gather x2, local copies, waits for them, and re-layouts, body(): jnp.take(arrived, filled[c * here:(c + 1) * here], axis=0, mode='clip')  5.99 us
  transfers between devices with their start and end apart: 17, of which 9 were waited for; matrix products, arithmetic and copies ran while one was open for 10% of the time, Pallas kernels for 26%

profile of v2, /device:TPU:1, one launch (start us, length us, event | category | flops | bytes accessed | tf_op | source)
XLA Modules:
  0.0 241.4 jit_solution(6420650707873589759)
XLA Ops:
  3.9 9.4 %all-to-all-start = ((s32[32,1,2]{2,1,0:T(1,128)}), s32[32,1,2]{2,1,0:T(1,128)S(1)}, u32[]{:S(2)}, u32[]{:S(2)}) async-start(s32[32,1,2]{2,1,0:T(1,128)} %bitcast), calls=%async_computation | async-start | bytes 32768 | tf_op jit(solution)/shard_map/all_to_all | solution.py:192
  14.5 5.8 %all-to-all-done = s32[32,1,2]{2,1,0:T(1,128)S(1)} async-done(((s32[32,1,2]{2,1,0:T(1,128)}), s32[32,1,2]{2,1,0:T(1,128)S(1)}, u32[]{:S(2)}, u32[]{:S(2)}) %all-to-all-start) | async-done | bytes 288 | tf_op jit(solution)/shard_map/all_to_all | solution.py:192
  21.6 3.3 %gather_fusion = bf16[64,128,128]{2,1,0:T(8,128)(2,1)} fusion(bf16[26,128,128]{2,1,0:T(8,128)(2,1)} %constant_dynamic-slice_fusion, s32[1024]{0:T(1024)S(1)} %pad_clamp_fusion.4), kind=kCustom, calls=%fused_computation | custom fusion | bytes 4194560 | tf_op jit(solution)/shard_map/jit(_take)/gather | solution.py:203
  24.9 5.1 %all-to-all-start.1 = ((bf16[32,2,128,128]{3,2,1,0:T(8,128)(2,1)}), bf16[32,2,128,128]{3,2,1,0:T(8,128)(2,1)}, u32[]{:S(2)}, u32[]{:S(2)}) async-start(bf16[32,2,128,128]{3,2,1,0:T(8,128)(2,1)} %bitcast.24), calls=%async_computation.1 | async-start | bytes 4194304 | tf_op jit(solution)/shard_map/all_to_all | solution.py:204
  30.2 28.3 %all-to-all-done.1 = bf16[32,2,128,128]{3,2,1,0:T(8,128)(2,1)} async-done(((bf16[32,2,128,128]{3,2,1,0:T(8,128)(2,1)}), bf16[32,2,128,128]{3,2,1,0:T(8,128)(2,1)}, u32[]{:S(2)}, u32[]{:S(2)}) %all-to-all-start.1) | async-done | bytes 2097184 | tf_op jit(solution)/shard_map/all_to_all | solution.py:204
  58.5 3.0 %gather_fusion.1 = bf16[16,128,128]{2,1,0:T(8,128)(2,1)} fusion(bf16[64,128,128]{2,1,0:T(8,128)(2,1)} %bitcast.2, s32[1024]{0:T(1024)S(1)} %get-tuple-element.80), kind=kCustom, calls=%fused_computation.1 | custom fusion | bytes 1048640 | tf_op jit(solution)/shard_map/jit(_take)/gather | solution.py:219
  61.5 2.9 %collective-permute-start.2 = (bf16[2048,128]{1,0:T(8,128)(2,1)}, bf16[2048,128]{1,0:T(8,128)(2,1)}, u32[]{:S(2)}, u32[]{:S(2)}) collective-permute-start(bf16[2048,128]{1,0:T(8,128)(2,1)} %bitcast.34), channel_id=1, source_target_pairs={{0,2},{1,3},{2,0},{3,1},{4,6},{5,7},{6,4},{7,5},{8,10},{9,11},{10,... | collective-permute-start | bytes 1572872 | tf_op jit(solution)/shard_map/ppermute | solution.py:214
  65.9 3.1 %pad_maximum_fusion = bf16[512,2048]{1,0:T(8,128)(2,1)} fusion(bf16[512,1024]{1,0:T(8,128)(2,1)} %param.11, bf16[512,1024]{1,0:T(8,128)(2,1)} %param.10), kind=kLoop, calls=%fused_computation.5 | loop fusion | flops 4194304 | bytes 4194304 | tf_op jit(solution)/shard_map/concatenate | solution.py:197
  69.0 3.6 %gather_fusion.2 = bf16[4,128,2048]{2,1,0:T(8,128)(2,1)} fusion(bf16[4,128,2048]{2,1,0:T(8,128)(2,1)} %bitcast.25, s32[1024]{0:T(1024)S(1)} %pad_clamp_fusion.2), kind=kCustom, calls=%fused_computation.2 | custom fusion | bytes 4194320 | tf_op jit(solution)/shard_map/jit(_take)/gather | solution.py:198
  72.6 4.0 %copy.41 = bf16[512,2048]{0,1:T(8,128)(2,1)} copy(bf16[512,2048]{1,0:T(8,128)(2,1)} %bitcast.21) | data formatting | bytes 4194304 | tf_op jit(solution)/shard_map/reshape | solution.py:199
  76.5 3.0 %gather_fusion.3 = bf16[16,128,128]{2,1,0:T(8,128)(2,1)} fusion(bf16[64,128,128]{2,1,0:T(8,128)(2,1)} %bitcast.2, s32[1024]{0:T(1024)S(1)} %get-tuple-element.79), kind=kCustom, calls=%fused_computation.3 | custom fusion | bytes 1048640 | tf_op jit(solution)/shard_map/jit(_take)/gather | solution.py:219
  79.5 8.2 %collective-permute-done.1.s2 = bf16[2048,128]{1,0:T(8,128)(2,1)} collective-permute-done((bf16[2048,128]{1,0:T(8,128)(2,1)}, bf16[2048,128]{1,0:T(8,128)(2,1)}, u32[]{:S(2)}, u32[]{:S(2)}) %collective-permute-start.1) | collective-permute-done | bytes 524320 | tf_op jit(solution)/shard_map/ppermute | solution.py:214
  88.4 2.9 %collective-permute-start.5 = (bf16[2048,128]{1,0:T(8,128)(2,1)}, bf16[2048,128]{1,0:T(8,128)(2,1)S(1)}, u32[]{:S(2)}, u32[]{:S(2)}) collective-permute-start(bf16[2048,128]{1,0:T(8,128)(2,1)} %bitcast.30), channel_id=1, source_target_pairs={{0,2},{1,3},{2,0},{3,1},{4,6},{5,7},{6,4},{7,5},{8,10},{9,11},{10,... | collective-permute-start | bytes 1572872 | tf_op jit(solution)/shard_map/ppermute | solution.py:214
  92.8 31.5 %shard_map.110 = (bf16[256,1024]{1,0:T(8,128)(2,1)}, bf16[256,1024]{1,0:T(8,128)(2,1)}, bf16[2048,128]{1,0:T(8,128)(2,1)}, bf16[2048,128]{1,0:T(8,128)(2,1)}, bf...) custom-call(s32[8]{0:T(128)} %get-tuple-element.73.counts, s32[4]{0:T(128)} %copy-done.5, ...), custom_call_target="tpu_custom_call" | custom-call | flops 24000000000 | bytes 4000000 | tf_op jit(solution)/shard_map/pallas_call | solution.py:113
  124.3 2.1 collective-permute-start.6
  127.6 29.9 %shard_map.111 = (bf16[256,1024]{1,0:T(8,128)(2,1)}, bf16[256,1024]{1,0:T(8,128)(2,1)}, bf16[2048,128]{1,0:T(8,128)(2,1)}, bf16[2048,128]{1,0:T(8,128)(2,1)}, bf...) custom-call(s32[8]{0:T(128)} %get-tuple-element.73.counts, s32[4]{0:T(128)} %copy-done.5, ...), custom_call_target="tpu_custom_call" | custom-call | flops 24000000000 | bytes 4000000 | tf_op jit(solution)/shard_map/pallas_call | solution.py:113
  157.6 2.3 dynamic-slice_bitcast_fusion
  159.9 2.0 collective-permute-start.9
  161.9 1.7 collective-permute-start.10
  164.5 2.9 %fusion = bf16[16,16,2048]{2,1,0:T(8,128)(2,1)} fusion(bf16[16,16,2048]{2,1,0:T(8,128)(2,1)} %collective-permute-done.9, bf16[16,2,16,2048]{3,2,1,0:T(8,128)(2,1)} %bitcast.27, s32[]{:T(128)S(6)} %select_n.107), kind=kLoop, calls=%fused_computation.7 | loop fusion | flops 2097152 | bytes 3145732 | tf_op jit(solution)/shard_map/convert_element_type | solution.py:251
  167.4 9.8 %collective-permute-done.10.d = bf16[2048,128]{1,0:T(8,128)(2,1)} collective-permute-done((bf16[2048,128]{1,0:T(8,128)(2,1)}, bf16[2048,128]{1,0:T(8,128)(2,1)}, u32[]{:S(2)}, u32[]{:S(2)}) %collective-permute-start.10) | collective-permute-done | bytes 524320 | tf_op jit(solution)/shard_map/ppermute | solution.py:214
  177.3 4.3 %all-to-all-start.3 = ((bf16[16,16,2048]{2,1,0:T(8,128)(2,1)}), bf16[16,16,2048]{2,1,0:T(8,128)(2,1)}, u32[]{:S(2)}, u32[]{:S(2)}) async-start(bf16[16,16,2048]{2,1,0:T(8,128)(2,1)} %fusion), calls=%async_computation.3 | async-start | bytes 2097152 | tf_op jit(solution)/shard_map/all_to_all | solution.py:261
  181.6 2.0 collective-permute-start.11
  184.1 1.8 add_convert_fusion
  185.8 10.0 %collective-permute-done.11.b = bf16[2048,128]{1,0:T(8,128)(2,1)S(1)} collective-permute-done((bf16[2048,128]{1,0:T(8,128)(2,1)}, bf16[2048,128]{1,0:T(8,128)(2,1)S(1)}, u32[]{:S(2)}, u32[]{:S(2)}) %collective-permute-start.11) | collective-permute-done | bytes 524320 | tf_op jit(solution)/shard_map/ppermute | solution.py:214
  195.8 1.9 collective-permute-done.12.c
  197.7 2.3 shard_map.112
  201.3 8.6 %all-to-all-start.2 = ((bf16[32,2,128,128]{3,2,1,0:T(8,128)(2,1)}), bf16[32,2,128,128]{3,2,1,0:T(8,128)(2,1)}, u32[]{:S(2)}, u32[]{:S(2)}) async-start(bf16[32,2,128,128]{3,2,1,0:T(8,128)(2,1)} %bitcast.19), calls=%async_computation.2 | async-start | bytes 4194304 | tf_op jit(solution)/shard_map/all_to_all | solution.py:265
  210.1 2.3 pad_maximum_fusion.1
  213.5 1.4 convert_reduce_fusion
  215.5 22.7 %all-to-all-done.2 = bf16[32,2,128,128]{3,2,1,0:T(8,128)(2,1)} async-done(((bf16[32,2,128,128]{3,2,1,0:T(8,128)(2,1)}), bf16[32,2,128,128]{3,2,1,0:T(8,128)(2,1)}, u32[]{:S(2)}, u32[]{:S(2)}) %all-to-all-start.2) | async-done | bytes 2097184 | tf_op jit(solution)/shard_map/all_to_all | solution.py:265
  238.2 3.2 %gather_fusion.4 = bf16[26,128,128]{2,1,0:T(8,128)(2,1)} fusion(bf16[64,128,128]{2,1,0:T(8,128)(2,1)} %bitcast.13, s32[1024]{0:T(1024)S(1)} %pad_clamp_fusion), kind=kCustom, calls=%fused_computation.4 | custom fusion | bytes 1704040 | tf_op jit(solution)/shard_map/jit(_take)/gather | solution.py:268
  (65 shorter events, 15.3 us)
Async XLA Ops:
  0.6 12.8 %copy-start = (bf16[26,128,512]{2,1,0:T(8,128)(2,1)S(1)}, bf16[26,128,512]{2,1,0:T(8,128)(2,1)}, u32[]{:S(2)}) copy-start(bf16[26,128,512]{2,1,0:T(8,128)(2,1)} %param.9) | copy-start | bytes 10223620
  3.9 16.3 %all-to-all-start = ((s32[32,1,2]{2,1,0:T(1,128)}), s32[32,1,2]{2,1,0:T(1,128)S(1)}, u32[]{:S(2)}, u32[]{:S(2)}) async-start(s32[32,1,2]{2,1,0:T(1,128)} %bitcast), calls=%async_computation | async-start | bytes 32768 | tf_op jit(solution)/shard_map/all_to_all | solution.py:192
  24.9 41.0 %copy-start.7 = (s32[4]{0:T(128)S(1)}, s32[4]{0:T(128)}, u32[]{:S(2)}) copy-start(s32[4]{0:T(128)} %constant.78.clone) | copy-start | bytes 52
  24.9 33.6 %all-to-all-start.1 = ((bf16[32,2,128,128]{3,2,1,0:T(8,128)(2,1)}), bf16[32,2,128,128]{3,2,1,0:T(8,128)(2,1)}, u32[]{:S(2)}, u32[]{:S(2)}) async-start(bf16[32,2,128,128]{3,2,1,0:T(8,128)(2,1)} %bitcast.24), calls=%async_computation.1 | async-start | bytes 4194304 | tf_op jit(solution)/shard_map/all_to_all | solution.py:204
  61.5 18.1 %collective-permute-start.2 = (bf16[2048,128]{1,0:T(8,128)(2,1)}, bf16[2048,128]{1,0:T(8,128)(2,1)}, u32[]{:S(2)}, u32[]{:S(2)}) collective-permute-start(bf16[2048,128]{1,0:T(8,128)(2,1)} %bitcast.34), channel_id=1, source_target_pairs={{0,2},{1,3},{2,0},{3,1},{4,6},{5,7},{6,4},{7,5},{8,10},{9,11},{10,... | collective-permute-start | bytes 1572872 | tf_op jit(solution)/shard_map/ppermute | solution.py:214
  64.4 23.3 %collective-permute-start.1 = (bf16[2048,128]{1,0:T(8,128)(2,1)}, bf16[2048,128]{1,0:T(8,128)(2,1)}, u32[]{:S(2)}, u32[]{:S(2)}) collective-permute-start(bf16[2048,128]{1,0:T(8,128)(2,1)} %bitcast.35), channel_id=1, source_target_pairs={{0,3},{1,0},{2,1},{3,2},{4,7},{5,4},{6,5},{7,6},{8,11},{9,8},{10,9... | collective-permute-start | bytes 1572872 | tf_op jit(solution)/shard_map/ppermute | solution.py:214
  65.2 23.2 %collective-permute-start = (bf16[2048,128]{1,0:T(8,128)(2,1)}, bf16[2048,128]{1,0:T(8,128)(2,1)}, u32[]{:S(2)}, u32[]{:S(2)}) collective-permute-start(bf16[2048,128]{1,0:T(8,128)(2,1)} %bitcast.36), channel_id=1, source_target_pairs={{0,1},{1,2},{2,3},{3,0},{4,5},{5,6},{6,7},{7,4},{8,9},{9,10},{10,1... | collective-permute-start | bytes 1572872 | tf_op jit(solution)/shard_map/ppermute | solution.py:214
  65.9 3.1 %copy-start.5 = (s32[4]{0:T(128)}, s32[4]{0:T(128)S(1)}, u32[]{:S(2)}) copy-start(s32[4]{0:T(128)S(1)} %and_select_fusion.2.quarters) | copy-start | bytes 52
  88.4 35.9 %collective-permute-start.5 = (bf16[2048,128]{1,0:T(8,128)(2,1)}, bf16[2048,128]{1,0:T(8,128)(2,1)S(1)}, u32[]{:S(2)}, u32[]{:S(2)}) collective-permute-start(bf16[2048,128]{1,0:T(8,128)(2,1)} %bitcast.30), channel_id=1, source_target_pairs={{0,2},{1,3},{2,0},{3,1},{4,6},{5,7},{6,4},{7,5},{8,10},{9,11},{10,... | collective-permute-start | bytes 1572872 | tf_op jit(solution)/shard_map/ppermute | solution.py:214
  91.3 33.0 %collective-permute-start.4 = (bf16[2048,128]{1,0:T(8,128)(2,1)}, bf16[2048,128]{1,0:T(8,128)(2,1)}, u32[]{:S(2)}, u32[]{:S(2)}) collective-permute-start(bf16[2048,128]{1,0:T(8,128)(2,1)} %bitcast.31), channel_id=1, source_target_pairs={{0,3},{1,0},{2,1},{3,2},{4,7},{5,4},{6,5},{7,6},{8,11},{9,8},{10,9... | collective-permute-start | bytes 1572872 | tf_op jit(solution)/shard_map/ppermute | solution.py:214
  92.1 32.2 %collective-permute-start.3 = (bf16[2048,128]{1,0:T(8,128)(2,1)}, bf16[2048,128]{1,0:T(8,128)(2,1)}, u32[]{:S(2)}, u32[]{:S(2)}) collective-permute-start(bf16[2048,128]{1,0:T(8,128)(2,1)} %bitcast.32), channel_id=1, source_target_pairs={{0,1},{1,2},{2,3},{3,0},{4,5},{5,6},{6,7},{7,4},{8,9},{9,10},{10,1... | collective-permute-start | bytes 1572872 | tf_op jit(solution)/shard_map/ppermute | solution.py:214
  124.2 3.4 %copy-start.6 = (bf16[2048,128]{1,0:T(8,128)(2,1)}, bf16[2048,128]{1,0:T(8,128)(2,1)S(1)}, u32[]{:S(2)}) copy-start(bf16[2048,128]{1,0:T(8,128)(2,1)S(1)} %collective-permute-done.5.s3) | copy-start | bytes 1572868
  124.3 33.3 %collective-permute-start.6 = (bf16[2048,128]{1,0:T(8,128)(2,1)}, bf16[2048,128]{1,0:T(8,128)(2,1)}, u32[]{:S(2)}, u32[]{:S(2)}) collective-permute-start(bf16[2048,128]{1,0:T(8,128)(2,1)} %get-tuple-element.44), channel_id=1, source_target_pairs={{0,3},{1,0},{2,1},{3,2},{4,7},{5,4},{6,5},{7,6},{8,11},{9,8},{10,9... | collective-permute-start | bytes 1572872 | tf_op jit(solution)/shard_map/ppermute | solution.py:214
  126.3 31.2 %collective-permute-start.7 = (bf16[2048,128]{1,0:T(8,128)(2,1)}, bf16[2048,128]{1,0:T(8,128)(2,1)}, u32[]{:S(2)}, u32[]{:S(2)}) collective-permute-start(bf16[2048,128]{1,0:T(8,128)(2,1)} %get-tuple-element.45), channel_id=1, source_target_pairs={{0,1},{1,2},{2,3},{3,0},{4,5},{5,6},{6,7},{7,4},{8,9},{9,10},{10,1... | collective-permute-start | bytes 1572872 | tf_op jit(solution)/shard_map/ppermute | solution.py:214
  126.3 31.2 %collective-permute-start.8 = (bf16[2048,128]{1,0:T(8,128)(2,1)}, bf16[2048,128]{1,0:T(8,128)(2,1)}, u32[]{:S(2)}, u32[]{:S(2)}) collective-permute-start(bf16[2048,128]{1,0:T(8,128)(2,1)} %get-tuple-element.46), channel_id=1, source_target_pairs={{0,2},{1,3},{2,0},{3,1},{4,6},{5,7},{6,4},{7,5},{8,10},{9,11},{10,... | collective-permute-start | bytes 1572872 | tf_op jit(solution)/shard_map/ppermute | solution.py:214
  159.9 4.7 %collective-permute-start.9 = (bf16[16,16,2048]{2,1,0:T(8,128)(2,1)}, bf16[16,16,2048]{2,1,0:T(8,128)(2,1)}, u32[]{:S(2)}, u32[]{:S(2)}) collective-permute-start(bf16[16,16,2048]{2,1,0:T(8,128)(2,1)} %dynamic-slice_bitcast_fusion), channel_id=1, source_target_pairs={{0,4},{4,0},{8,12},{12,8},{16,20},{20,16},{24,28},{28,24},{32,36},... | collective-permute-start | bytes 3145736 | tf_op jit(solution)/shard_map/ppermute | solution.py:250
  161.9 15.4 %collective-permute-start.10 = (bf16[2048,128]{1,0:T(8,128)(2,1)}, bf16[2048,128]{1,0:T(8,128)(2,1)}, u32[]{:S(2)}, u32[]{:S(2)}) collective-permute-start(bf16[2048,128]{1,0:T(8,128)(2,1)} %get-tuple-element.56), channel_id=1, source_target_pairs={{0,2},{1,3},{2,0},{3,1},{4,6},{5,7},{6,4},{7,5},{8,10},{9,11},{10,... | collective-permute-start | bytes 1572872 | tf_op jit(solution)/shard_map/ppermute | solution.py:214
  177.3 24.0 %all-to-all-start.3 = ((bf16[16,16,2048]{2,1,0:T(8,128)(2,1)}), bf16[16,16,2048]{2,1,0:T(8,128)(2,1)}, u32[]{:S(2)}, u32[]{:S(2)}) async-start(bf16[16,16,2048]{2,1,0:T(8,128)(2,1)} %fusion), calls=%async_computation.3 | async-start | bytes 2097152 | tf_op jit(solution)/shard_map/all_to_all | solution.py:261
  181.6 16.1 %copy-start.2 = (bf16[2048,128]{1,0:T(8,128)(2,1)S(1)}, bf16[2048,128]{1,0:T(8,128)(2,1)}, u32[]{:S(2)}) copy-start(bf16[2048,128]{1,0:T(8,128)(2,1)} %get-tuple-element.52.a) | copy-start | bytes 1572868
  181.6 14.2 %collective-permute-start.11 = (bf16[2048,128]{1,0:T(8,128)(2,1)}, bf16[2048,128]{1,0:T(8,128)(2,1)S(1)}, u32[]{:S(2)}, u32[]{:S(2)}) collective-permute-start(bf16[2048,128]{1,0:T(8,128)(2,1)} %get-tuple-element.57), channel_id=1, source_target_pairs={{0,3},{1,0},{2,1},{3,2},{4,7},{5,4},{6,5},{7,6},{8,11},{9,8},{10,9... | collective-permute-start | bytes 1572872 | tf_op jit(solution)/shard_map/ppermute | solution.py:214
  183.6 14.1 %collective-permute-start.12 = (bf16[2048,128]{1,0:T(8,128)(2,1)}, bf16[2048,128]{1,0:T(8,128)(2,1)S(1)}, u32[]{:S(2)}, u32[]{:S(2)}) collective-permute-start(bf16[2048,128]{1,0:T(8,128)(2,1)} %get-tuple-element.58), channel_id=1, source_target_pairs={{0,1},{1,2},{2,3},{3,0},{4,5},{5,6},{6,7},{7,4},{8,9},{9,10},{10,1... | collective-permute-start | bytes 1572872 | tf_op jit(solution)/shard_map/ppermute | solution.py:214
  200.0 1.3 copy-start.1
  201.3 36.9 %all-to-all-start.2 = ((bf16[32,2,128,128]{3,2,1,0:T(8,128)(2,1)}), bf16[32,2,128,128]{3,2,1,0:T(8,128)(2,1)}, u32[]{:S(2)}, u32[]{:S(2)}) async-start(bf16[32,2,128,128]{3,2,1,0:T(8,128)(2,1)} %bitcast.19), calls=%async_computation.2 | async-start | bytes 4194304 | tf_op jit(solution)/shard_map/all_to_all | solution.py:265
  210.0 2.5 %copy-start.3 = (bf16[256,1024]{1,0:T(8,128)(2,1)S(1)}, bf16[256,1024]{1,0:T(8,128)(2,1)}, u32[]{:S(2)}) copy-start(bf16[256,1024]{1,0:T(8,128)(2,1)} %get-tuple-element.37) | copy-start | bytes 1572868
  210.0 2.5 %copy-start.4 = (bf16[256,1024]{1,0:T(8,128)(2,1)S(1)}, bf16[256,1024]{1,0:T(8,128)(2,1)}, u32[]{:S(2)}) copy-start(bf16[256,1024]{1,0:T(8,128)(2,1)} %get-tuple-element.38) | copy-start | bytes 1572868
